TPU v7x, 32 devices: a whole 2x2x4 slice. The times are simulated.
32 devices in a mesh: dp: 8 (over z, x), tensor: 4 (over y, core).
Axes of the slice: x: 2, y: 2, z: 4, core: 2. Of those that a mesh axis runs over, the one named last changes fastest.
Arguments:
- resid_in: bfloat16 [4, 1024, 1024], P(None, ('dp', 'tensor')), may hold values from -6 to 6
- segment_ids: int32 [4, 1024], replicated, may hold values from 0 to 64, as said below
- out_grad: bfloat16 [4, 1024, 1024], P(None, ('dp', 'tensor')), may hold values from -6 to 6
- input_gain: float32 [1024], replicated, may hold values from 0.5 to 1.5
- ffn_gain: float32 [1024], replicated, may hold values from 0.5 to 1.5
- query_weight: bfloat16 [1024, 512], P('dp', 'tensor'), may hold values from -0.1875 to 0.1875
- keyvalue_weight: bfloat16 [1024, 2, 128], P('dp'), may hold values from -0.1875 to 0.1875
- attention_output_weight: bfloat16 [512, 1024], P('tensor', 'dp'), may hold values from -1 to 1
- mixer_input_weight: bfloat16 [1024, 2, 1536], P('dp', None, 'tensor'), may hold values from -0.1875 to 0.1875
- state_input_weight: bfloat16 [1024, 256], P('dp'), may hold values from -0.1875 to 0.1875
- step_weight: bfloat16 [1024, 24], P('dp', 'tensor'), may hold values from -0.1875 to 0.1875
- conv_mixer: float32 [4, 1536], P(None, 'tensor'), may hold values from -3 to 3
- conv_mixer_bias: float32 [1536], P('tensor'), may hold values from -2 to 2
- conv_state: float32 [4, 256], replicated, may hold values from -3 to 3
- conv_state_bias: float32 [256], replicated, may hold values from -2 to 2
- step_bias: float32 [24], P('tensor'), may hold values from -1.5 to 0.5
- decay_log: float32 [24], P('tensor'), may hold values from -12 to -2
- skip_gain: float32 [24], P('tensor'), may hold values from 0.5 to 1.5
- mixer_gain: float32 [1536], P('tensor'), may hold values from 0.5 to 1.5
- mixer_output_weight: bfloat16 [1536, 1024], P('tensor', 'dp'), may hold values from -0.15625 to 0.15625
- gate_up_weight: bfloat16 [1024, 2, 2048], P('dp', None, 'tensor'), may hold values from -0.1875 to 0.1875
- down_weight: bfloat16 [2048, 1024], P('tensor', 'dp'), may hold values from -0.125 to 0.125
Outputs:
- block_out: bfloat16 [4, 1024, 1024], P(None, ('dp', 'tensor'))
- resid_grad: float32 [4, 1024, 1024], P(None, ('dp', 'tensor'))
- input_gain_grad: float32 [1024], replicated
- ffn_gain_grad: float32 [1024], replicated
- w_query_grad: float32 [1024, 512], P('dp', 'tensor')
- w_keyval_grad: float32 [1024, 2, 128], P('dp')
- w_attn_out_grad: float32 [512, 1024], P('tensor', 'dp')
- w_mixer_in_grad: float32 [1024, 2, 1536], P('dp', None, 'tensor')
- w_state_in_grad: float32 [1024, 256], P('dp')
- w_step_grad: float32 [1024, 24], P('dp', 'tensor')
- conv_mixer_grad: float32 [4, 1536], P(None, 'tensor')
- conv_mixer_bias_grad: float32 [1536], P('tensor')
- conv_state_grad: float32 [4, 256], replicated
- conv_state_bias_grad: float32 [256], replicated
- step_bias_grad: float32 [24], P('tensor')
- decay_log_grad: float32 [24], P('tensor')
- skip_gain_grad: float32 [24], P('tensor')
- mixer_gain_grad: float32 [1536], P('tensor')
- w_mixer_out_grad: float32 [1536, 1024], P('tensor', 'dp')
- w_gate_up_grad: float32 [1024, 2, 2048], P('dp', None, 'tensor')
- w_down_grad: float32 [2048, 1024], P('tensor', 'dp')
Inputs may be any that keep to these rules, and one draw needn't show every extreme that they name: `segment_ids`: in each sequence the numbers start at 0 and rise by 0 or 1 from one token to the next; equal numbers mark one document. Some sequence is one document from its first token into its last 128 tokens, where 128 // 2 of those tokens each start a new document.
All inputs are finite; a program needn't handle non-finite values.
Results may differ from a plain program's by a relative error of at most 0.035.
Values may be sent and summed in bfloat16 or wider, within the bound.
A program may use at most 320 MiB of HBM per device.

v0:
```python
from functools import partial
import math

import jax
import jax.numpy as jnp
import numpy as np
from jax import lax
from jax.experimental import pallas as pl
from jax.experimental.pallas import tpu as pltpu
from jax.sharding import PartitionSpec as P

KVH = 2
EPSILON = 1e-05
ROTARY_BASE = 100000000000.0
MASKED = -1e30
MATMUL_EXACTNESS = lax.Precision.HIGHEST
LANES = 128
F32 = jnp.float32
BF16 = jnp.bfloat16
VMEM_BYTES = 63 * 2**20
JOINED_TOKENS = 4096


def dot_nn(a, b):
    return lax.dot_general(a, b, (((1,), (0,)), ((), ())), preferred_element_type=F32)


def dot_nt(a, b):
    return lax.dot_general(a, b, (((1,), (1,)), ((), ())), preferred_element_type=F32)


def dot_tn(a, b):
    return lax.dot_general(a, b, (((0,), (0,)), ((), ())), preferred_element_type=F32)


def remote(src, dst, send_sem, recv_sem, where):
    return pltpu.make_async_remote_copy(
        src_ref=src,
        dst_ref=dst,
        send_sem=send_sem,
        recv_sem=recv_sem,
        device_id=where,
        device_id_type=pl.DeviceIdType.MESH,
    )


def add_into(ref, *others):
    total = ref[...].astype(F32)
    for other in others:
        total = total + other[...].astype(F32)
    ref[...] = total.astype(BF16)


class Place:
    def __init__(self, devices):
        self.devices = devices
        self.lines = devices // 2
        self.dp = lax.axis_index("dp")
        self.t = lax.axis_index("tensor")
        self.z = lax.div(self.dp, 2)
        self.p = lax.rem(self.dp, 2)
        self.pair = self.dp + 1 - 2 * self.p
        self.t_near = self.t + 1 - 2 * lax.rem(self.t, 2)
        self.t_far = lax.rem(self.t + 2, 4)
        self.t_both = lax.rem(self.t_near + 2, 4)
        self.first = self.z == 0
        self.last = self.z == self.lines - 1

    def flips(self):
        bit = 1
        while bit < self.devices:
            yield self.dp + bit - 2 * bit * lax.rem(lax.div(self.dp, bit), 2)
            bit *= 2


class LineGather:
    def __init__(self, place, view, recv, right, left, pair, causal=False):
        self.at, self.view = place, view
        self.causal = causal
        self.recv, self.right, self.left, self.side = recv, right, left, pair

    def copy(self, block, sem, where):
        ref = self.view(block)
        return remote(ref, ref, sem, self.recv.at[block], where)

    def send_right(self, zz):
        return self.copy(zz * 2 + self.at.p, self.right.at[zz], {"dp": self.at.dp + 2})

    def send_left(self, zz):
        return self.copy(zz * 2 + self.at.p, self.left.at[zz], {"dp": self.at.dp - 2})

    def send_pair(self, zz):
        return self.copy(zz * 2 + self.at.p, self.side.at[zz], {"dp": self.at.pair})

    def arrived(self, block):
        self.copy(block, self.side.at[0], {"dp": self.at.pair}).wait_recv()

    def start(self):
        at = self.at
        pl.when(jnp.logical_not(at.last))(lambda: self.send_right(at.z).start())
        if not self.causal:
            pl.when(jnp.logical_not(at.first))(lambda: self.send_left(at.z).start())
        self.send_pair(at.z).start()

    def step(self, s):
        at = self.at
        low, high = at.z - 1 - s, at.z + 1 + s

        @pl.when(low >= 0)
        def _():
            self.arrived(low * 2 + at.p)
            pl.when(jnp.logical_not(at.last))(lambda: self.send_right(low).start())
            self.send_pair(low).start()

        if self.causal:
            return

        @pl.when(high < at.lines)
        def _():
            self.arrived(high * 2 + at.p)
            pl.when(jnp.logical_not(at.first))(lambda: self.send_left(high).start())
            self.send_pair(high).start()

    def finish(self):
        at = self.at

        @pl.loop(0, at.z + 1 if self.causal else at.lines)
        def _(zz):
            self.arrived(zz * 2 + 1 - at.p)

    def drain(self):
        at = self.at

        @pl.loop(0, at.z + 1 if self.causal else at.lines)
        def _(zz):
            self.send_pair(zz).wait_send()

            @pl.when(jnp.logical_and(zz <= at.z, jnp.logical_not(at.last)))
            def _():
                self.send_right(zz).wait_send()

            if self.causal:
                return

            @pl.when(jnp.logical_and(zz >= at.z, jnp.logical_not(at.first)))
            def _():
                self.send_left(zz).wait_send()


class CrossGather:
    def __init__(self, place, view, recv, right, left, pair):
        self.at, self.view = place, view
        self.recv, self.right, self.left, self.side = recv, right, left, pair

    def copy(self, block, sem, where):
        ref = self.view(block)
        return remote(ref, ref, sem, self.recv.at[block], where)

    def send_right(self, block):
        return self.copy(block, self.right.at[block], {"dp": self.at.dp + 2})

    def send_left(self, block):
        return self.copy(block, self.left.at[block], {"dp": self.at.dp - 2})

    def send_pair(self):
        return self.copy(self.at.dp, self.side.at[0], {"dp": self.at.pair})

    def arrived(self, block):
        self.copy(block, self.side.at[0], {"dp": self.at.pair}).wait_recv()

    def onward(self, block, right, left):
        at = self.at
        if right:
            pl.when(jnp.logical_not(at.last))(lambda: self.send_right(block).start())
        if left:
            pl.when(jnp.logical_not(at.first))(lambda: self.send_left(block).start())

    def start(self):
        self.send_pair().start()
        self.onward(self.at.dp, True, True)

    def begin(self):
        self.arrived(self.at.pair)
        self.onward(self.at.pair, True, True)

    def step(self, s):
        at = self.at
        low, high = at.z - 1 - s, at.z + 1 + s
        for q in (at.p, 1 - at.p):

            @pl.when(low >= 0)
            def _():
                self.arrived(low * 2 + q)
                self.onward(low * 2 + q, True, False)

            @pl.when(high < at.lines)
            def _():
                self.arrived(high * 2 + q)
                self.onward(high * 2 + q, False, True)

    def finish(self):
        pass

    def drain(self):
        at = self.at
        self.send_pair().wait_send()

        @pl.loop(0, at.devices)
        def _(block):
            zz = lax.div(block, 2)

            @pl.when(jnp.logical_and(zz <= at.z, jnp.logical_not(at.last)))
            def _():
                self.send_right(block).wait_send()

            @pl.when(jnp.logical_and(zz >= at.z, jnp.logical_not(at.first)))
            def _():
                self.send_left(block).wait_send()


class LineScatter:
    def __init__(self, place, part, got, right, left, sems, causal=False):
        self.at, self.part = place, part
        self.got, self.right, self.left = got, right, left
        self.causal = causal
        (
            self.pair_send,
            self.pair_recv,
            self.right_send,
            self.right_recv,
            self.left_send,
            self.left_recv,
        ) = sems

    def pair_copy(self, zz):
        src = self.part(zz * 2 + 1 - self.at.p)
        return remote(
            src, self.got(zz), self.pair_send.at[zz], self.pair_recv.at[zz], {"dp": self.at.pair}
        )

    def right_copy(self, zz):
        src = self.part(zz * 2 + self.at.p)
        return remote(
            src,
            self.right(zz),
            self.right_send.at[zz],
            self.right_recv.at[zz],
            {"dp": self.at.dp + 2},
        )

    def left_copy(self, zz):
        src = self.part(zz * 2 + self.at.p)
        return remote(
            src, self.left(zz), self.left_send.at[zz], self.left_recv.at[zz], {"dp": self.at.dp - 2}
        )

    def start(self):
        at = self.at

        @pl.loop(0, at.z + 1 if self.causal else at.lines)
        def _(i):
            self.pair_copy(i if self.causal else at.lines - 1 - i).start()

    def step(self, i):
        at = self.at
        high, low = at.lines - 1 - i, i
        if self.causal:
            self.step_low(low)
            return

        @pl.when(at.z < at.lines // 2)
        def _():
            self.step_high(high)
            self.step_low(low)

        @pl.when(at.z >= at.lines // 2)
        def _():
            self.step_low(low)
            self.step_high(high)

    def step_high(self, high):
        at = self.at

        @pl.when(high > at.z)
        def _():
            self.pair_copy(high).wait_recv()
            ref = self.part(high * 2 + at.p)

            @pl.when(at.first)
            def _():
                add_into(ref, self.got(high))

            @pl.when(jnp.logical_not(at.first))
            def _():
                self.right_copy(high).wait_recv()
                add_into(ref, self.got(high), self.right(high))

            self.right_copy(high).start()

    def step_low(self, low):
        at = self.at

        @pl.when(low < at.z)
        def _():
            self.pair_copy(low).wait_recv()
            ref = self.part(low * 2 + at.p)

            @pl.when(at.last)
            def _():
                add_into(ref, self.got(low))

            @pl.when(jnp.logical_not(at.last))
            def _():
                self.left_copy(low).wait_recv()
                add_into(ref, self.got(low), self.left(low))

            self.left_copy(low).start()

    def finish(self, out):
        at = self.at
        self.pair_copy(at.z).wait_recv()
        out[...] = self.part(at.dp)[...].astype(F32) + self.got(at.z)[...].astype(F32)

        if not self.causal:

            @pl.when(jnp.logical_not(at.first))
            def _():
                self.right_copy(at.z).wait_recv()
                out[...] += self.right(at.z)[...].astype(F32)

        @pl.when(jnp.logical_not(at.last))
        def _():
            self.left_copy(at.z).wait_recv()
            out[...] += self.left(at.z)[...].astype(F32)

    def drain(self):
        at = self.at

        @pl.loop(0, at.z + 1 if self.causal else at.lines)
        def _(zz):
            self.pair_copy(zz).wait_send()
            if not self.causal:
                pl.when(zz > at.z)(lambda: self.right_copy(zz).wait_send())
            pl.when(zz < at.z)(lambda: self.left_copy(zz).wait_send())

    def run_causal(self, out):
        @pl.loop(0, self.at.lines - 1)
        def _(s):
            self.step(s)

        self.finish(out)


class CrossScatter:
    def __init__(self, place, part, got, line, sems):
        self.at, self.part, self.got, self.line = place, part, got, line
        self.pair_send, self.pair_recv = sems[0].at[0], sems[0].at[1]
        self.right_send, self.right_recv, self.left_send, self.left_recv = sems[1:]

    def right_copy(self, zz, q):
        block = zz * 2 + q
        return remote(
            self.part(block),
            self.line(zz + 1, q),
            self.right_send.at[block],
            self.right_recv.at[block],
            {"dp": self.at.dp + 2},
        )

    def left_copy(self, zz, q):
        block = zz * 2 + q
        return remote(
            self.part(block),
            self.line(zz, q),
            self.left_send.at[block],
            self.left_recv.at[block],
            {"dp": self.at.dp - 2},
        )

    def pair_copy(self):
        return remote(
            self.part(self.at.pair), self.got, self.pair_send, self.pair_recv, {"dp": self.at.pair}
        )

    def start(self):
        pass

    def step(self, i):
        at = self.at
        high, low = at.lines - 1 - i, i

        @pl.when(at.z < at.lines // 2)
        def _():
            self.step_high(high)
            self.step_low(low)

        @pl.when(at.z >= at.lines // 2)
        def _():
            self.step_low(low)
            self.step_high(high)

    def step_high(self, high):
        at = self.at

        @pl.when(high > at.z)
        def _():
            for q in (1 - at.p, at.p):

                @pl.when(jnp.logical_not(at.first))
                def _():
                    self.right_copy(high, q).wait_recv()
                    add_into(self.part(high * 2 + q), self.line(high + 1, q))

                self.right_copy(high, q).start()

    def step_low(self, low):
        at = self.at

        @pl.when(low < at.z)
        def _():
            for q in (1 - at.p, at.p):

                @pl.when(jnp.logical_not(at.last))
                def _():
                    self.left_copy(low, q).wait_recv()
                    add_into(self.part(low * 2 + q), self.line(low, q))

                self.left_copy(low, q).start()

    def join(self):
        at = self.at
        for q in (1 - at.p, at.p):
            ref = self.part(at.z * 2 + q)

            @pl.when(jnp.logical_not(at.first))
            def _():
                self.right_copy(at.z, q).wait_recv()
                add_into(ref, self.line(at.z + 1, q))

            @pl.when(jnp.logical_not(at.last))
            def _():
                self.left_copy(at.z, q).wait_recv()
                add_into(ref, self.line(at.z, q))

            if q is not at.p:
                self.pair_copy().start()

    def finish(self, out):
        self.pair_copy().wait_recv()
        out[...] = self.part(self.at.dp)[...].astype(F32) + self.got[...].astype(F32)

    def drain(self):
        at = self.at
        self.pair_copy().wait_send()

        @pl.loop(0, at.devices)
        def _(block):
            zz, q = lax.div(block, 2), lax.rem(block, 2)
            pl.when(zz > at.z)(lambda: self.right_copy(zz, q).wait_send())
            pl.when(zz < at.z)(lambda: self.left_copy(zz, q).wait_send())


class RowGather:
    def __init__(self, place, view, send, recv):
        self.at, self.view, self.send, self.recv = place, view, send, recv

    def copy(self, rank, chunk, sem, near):
        ref = self.view(rank, chunk)
        where = {"tensor": self.at.t_near if near else self.at.t_far}
        return remote(ref, ref, self.send.at[chunk, sem], self.recv.at[chunk, rank], where)

    def start(self, chunk):
        self.copy(self.at.t, chunk, 0, False).start()
        self.copy(self.at.t, chunk, 1, True).start()

    def forward(self, chunk):
        self.copy(self.at.t_far, chunk, 2, False).wait_recv()
        self.copy(self.at.t_far, chunk, 2, True).start()

    def finish(self, chunk):
        self.copy(self.at.t_near, chunk, 1, True).wait_recv()
        self.copy(self.at.t_both, chunk, 2, True).wait_recv()

    def drain(self, chunk):
        self.copy(self.at.t, chunk, 0, False).wait_send()
        self.copy(self.at.t, chunk, 1, True).wait_send()
        self.copy(self.at.t_far, chunk, 2, True).wait_send()


class RowScatter:
    def __init__(self, place, view, near_buf, far_buf, send, recv):
        self.at, self.view = place, view
        self.near_buf, self.far_buf = near_buf, far_buf
        self.send, self.recv = send, recv

    def near_copy(self, chunk, which):
        rank = self.at.t_both if which else self.at.t_near
        return remote(
            self.view(rank, chunk),
            self.near_buf(which, chunk),
            self.send.at[chunk, which],
            self.recv.at[chunk, which],
            {"tensor": self.at.t_near},
        )

    def far_copy(self, chunk):
        return remote(
            self.view(self.at.t_far, chunk),
            self.far_buf(chunk),
            self.send.at[chunk, 2],
            self.recv.at[chunk, 2],
            {"tensor": self.at.t_far},
        )

    def start(self, chunk):
        self.near_copy(chunk, 1).start()
        self.near_copy(chunk, 0).start()

    def middle(self, chunk):
        self.near_copy(chunk, 1).wait_recv()
        ref = self.view(self.at.t_far, chunk)
        ref[...] = (ref[...].astype(F32) + self.near_buf(1, chunk)[...].astype(F32)).astype(BF16)
        self.far_copy(chunk).start()

    def finish(self, chunk):
        self.near_copy(chunk, 0).wait_recv()
        total = self.view(self.at.t, chunk)[...].astype(F32) + self.near_buf(0, chunk)[
            ...
        ].astype(F32)
        self.far_copy(chunk).wait_recv()
        return total + self.far_buf(chunk)[...].astype(F32)

    def drain(self, chunk):
        self.near_copy(chunk, 0).wait_send()
        self.near_copy(chunk, 1).wait_send()
        self.far_copy(chunk).wait_send()


def line_gather_sems(devices):
    dma = pltpu.SemaphoreType.DMA
    return [dma((devices,)), dma((devices // 2,)), dma((devices // 2,)), dma((devices // 2,))]


def line_scatter_sems(devices):
    return [pltpu.SemaphoreType.DMA((devices // 2,)) for _ in range(6)]


def rms_rows(values, gain):
    return values * lax.rsqrt(jnp.mean(values * values, -1, keepdims=True) + EPSILON) * gain


def rms_rows_grad(values, gain, grad):
    scale = lax.rsqrt(jnp.mean(values * values, -1, keepdims=True) + EPSILON)
    term = grad * gain
    inner = jnp.mean(values * term, -1, keepdims=True)
    return scale * (term - values * (scale * scale * inner)), grad * values * scale


def ffn_kernel(devices, layout, *refs, joined=None):
    (
        x_ref, a_ref, og_ref, ogl_ref, gain_ref, w_any, dn_in,
        out_ref, gh_ref, gb, nf, act, dgu, gain_grad,
        part, part2, near1, far1, near2, far2, near3, far3, hid,
        w_ref, w_dn, w_sem, send, recv, *sems,
    ) = refs
    at = Place(devices)
    seqs, sub, width = x_ref.shape
    span = sub * 4
    half = seqs // 2
    rows = half * span
    first = layout["out"][0] if joined is None else 0
    out_w, gu_w = (pl.ds(layout[k][0] - first, layout[k][1]) for k in ("out", "gu"))
    ff = layout["down"][1]
    if joined is None:
        depth = dn_in.shape[1]
        load = pltpu.make_async_copy(w_any.at[:, pl.ds(first, w_ref.shape[1])], w_ref, w_sem)
        load.start()
        w_dn[pl.ds(pl.multiple_of(at.dp * depth, depth), depth), :] = dn_in[...].T
        Neighbours(at).greet()
    else:
        w_ref = w_any

    def down():
        return w_dn[...] if joined is None else w_ref[:, pl.ds(*layout["down"])]

    def rows_of(buf):
        def view(rank, chunk):
            return buf.at[pl.ds(chunk * half, half), pl.ds(pl.multiple_of(rank * sub, sub), sub), :]

        return view

    def parts_of(buf):
        return lambda which, chunk: buf.at[which, pl.ds(chunk * half, half)]

    def part_of(buf):
        return lambda chunk: buf.at[pl.ds(chunk * half, half)]

    branch = RowScatter(at, rows_of(part), parts_of(near1), part_of(far1), send.at[0], recv.at[0])
    ffn = RowScatter(at, rows_of(part2), parts_of(near2), part_of(far2), send.at[1], recv.at[1])
    back = RowScatter(at, rows_of(part), parts_of(near3), part_of(far3), send.at[2], recv.at[2])
    row_nf = RowGather(at, rows_of(nf), send.at[3], recv.at[3])
    row_gb = RowGather(at, rows_of(gb), send.at[4], recv.at[4])
    mine = pl.ds(pl.multiple_of(at.t * sub, sub), sub)
    gain = gain_ref[...].reshape(1, width)

    def seq_rows(chunk):
        return pl.ds(chunk * half, half)

    def tok_rows(chunk):
        return pl.ds(chunk * rows, rows)

    if joined is None:
        gather = LineGather(
            at, lambda block: w_dn.at[pl.ds(pl.multiple_of(block * depth, depth), depth), :], *sems
        )
        gather.start()
        load.wait()
        gather_step = gather.step
    else:
        joined.step(3, 2)
        gather_step = partial(joined.step, 4)
    for c in range(2):
        value = dot_nt(a_ref[tok_rows(c), :], w_ref[:, out_w])
        part[seq_rows(c)] = value.astype(BF16).reshape(half, span, width)
        branch.start(c)
    for c in range(2):
        branch.middle(c)
    gather_step(0)
    for c in range(2):
        hidden = x_ref[seq_rows(c)].astype(F32) + branch.finish(c)
        hid[seq_rows(c)] = hidden
        nf[seq_rows(c), mine, :] = rms_rows(hidden, gain).astype(BF16)
        row_nf.start(c)
    gather_step(1)
    if joined is not None:
        gather_step(2)
        joined.gathers[3].finish()
        joined.gathers[4].finish()
    for c in range(2):
        row_nf.forward(c)
    if joined is None:
        pl.loop(2, at.lines - 1)(lambda s: gather.step(s))
        gather.finish()
    for c in range(2):
        row_nf.finish(c)
        branch.drain(c)
        flat = nf[seq_rows(c)].reshape(rows, width)
        flat_og = og_ref[seq_rows(c)].reshape(rows, width)
        gate_up = dot_nn(flat, w_ref[:, gu_w])
        gate, up = gate_up[:, :ff], gate_up[:, ff:]
        sigmoid = jax.nn.sigmoid(gate)
        grad_act = dot_nn(flat_og, down())
        act[tok_rows(c), :] = (gate * sigmoid * up).astype(BF16)
        dgu[tok_rows(c), :ff] = (
            grad_act * up * sigmoid * (1.0 + gate * (1.0 - sigmoid))
        ).astype(BF16)
        dgu[tok_rows(c), ff:] = (grad_act * gate * sigmoid).astype(BF16)
        value = dot_nt(dgu[tok_rows(c), :], w_ref[:, gu_w])
        part[seq_rows(c)] = value.astype(BF16).reshape(half, span, width)
        back.start(c)
    for c in range(2):
        value = dot_nt(act[tok_rows(c), :], down())
        part2[seq_rows(c)] = value.astype(BF16).reshape(half, span, width)
    if joined is not None:
        joined.activations_ready()
    for c in range(2):
        back.middle(c)
    total = jnp.zeros((1, width), F32)
    for c in range(2):
        grad_hidden, terms = rms_rows_grad(hid[seq_rows(c)], gain, back.finish(c))
        total = total + jnp.sum(terms.reshape(half * sub, width), 0, keepdims=True)
        grad_hidden = grad_hidden + ogl_ref[seq_rows(c)].astype(F32)
        gh_ref[seq_rows(c)] = grad_hidden
        gb[seq_rows(c), mine, :] = grad_hidden.astype(BF16)
        row_gb.start(c)
        ffn.start(c)
    gain_grad[...] = total
    for c in range(2):
        row_gb.forward(c)
        ffn.middle(c)
    for c in range(2):
        out_ref[seq_rows(c)] = (hid[seq_rows(c)] + ffn.finish(c)).astype(BF16)
        row_gb.finish(c)
    def drain():
        for c in range(2):
            row_nf.drain(c)
            row_gb.drain(c)
            back.drain(c)
            ffn.drain(c)

    drain()
    if joined is None:
        gather.drain()


def ffn_specs(cfg):
    layout = cfg["layout"]
    seqs, sub, width = cfg["rows"]
    span = sub * 4
    tokens = seqs * span
    ff = layout["down"][1]
    dma = pltpu.SemaphoreType.DMA
    whole, own = (seqs, span, width), (seqs, sub, width)
    outs = (
        (own, BF16),
        (own, F32),
        (whole, BF16),
        (whole, BF16),
        ((tokens, ff), BF16),
        ((tokens, 2 * ff), BF16),
        ((1, width), F32),
    )
    buffers = [pltpu.VMEM(whole, BF16), pltpu.VMEM(whole, BF16)]
    buffers += [pltpu.VMEM((2,) + own, BF16), pltpu.VMEM(own, BF16)] * 3
    buffers += [pltpu.VMEM(own, F32)]
    weights = [
        pltpu.VMEM((width, layout["down"][0] - layout["out"][0]), BF16),
        pltpu.VMEM((width, ff), BF16),
        dma,
    ]
    sems = [dma((5, 2, 3)), dma((5, 2, 4))]
    return outs, buffers, weights, sems


def feed_forward(cfg, x, a, og, out_grad, gain, w_all, w_down):
    outs, buffers, weights, sems = ffn_specs(cfg)
    vmem = pl.BlockSpec(memory_space=pltpu.VMEM)
    return pl.pallas_call(
        partial(ffn_kernel, cfg["devices"], cfg["layout"]),
        out_shape=tuple(jax.ShapeDtypeStruct(*out) for out in outs),
        in_specs=[vmem] * 5 + [pl.BlockSpec(memory_space=pl.ANY), vmem],
        out_specs=(vmem,) * 7,
        scratch_shapes=buffers + weights + sems + line_gather_sems(cfg["devices"]),
        compiler_params=pltpu.CompilerParams(
            collective_id=1, has_side_effects=True, vmem_limit_bytes=VMEM_BYTES
        ),
        name="feed_forward",
    )(x, a, og, out_grad, gain, w_all, w_down)


def to_row(column):
    size = column.shape[0]
    eye = iota((size, size), 0) == iota((size, size), 1)
    return jnp.sum(jnp.where(eye, column, 0.0), 0, keepdims=True)


def to_column(row):
    size = row.shape[1]
    eye = iota((size, size), 0) == iota((size, size), 1)
    return jnp.sum(jnp.where(eye, row, 0.0), 1, keepdims=True)


def iota(shape, dim):
    return lax.broadcasted_iota(jnp.int32, shape, dim)


def spread(columns, heads, head_dim):
    rows = columns.shape[0]
    lane = iota((rows, LANES), 1)
    blocks = []
    for first in range(0, heads, LANES // head_dim):
        block = jnp.broadcast_to(columns[:, first : first + 1], (rows, LANES))
        for k in range(1, LANES // head_dim):
            block = jnp.where(lane >= k * head_dim, columns[:, first + k : first + k + 1], block)
        blocks.append(block)
    return jnp.concatenate(blocks, 1)


def head_sums(values, heads, head_dim):
    rows = values.shape[0]
    lane = iota((rows, LANES), 1)
    out = jnp.zeros((rows, LANES), F32)
    per = LANES // head_dim
    for h in range(heads):
        block = values[:, h // per * LANES : (h // per + 1) * LANES]
        inside = jnp.logical_and(lane >= h % per * head_dim, lane < (h % per + 1) * head_dim)
        total = jnp.sum(jnp.where(inside, block, 0.0), 1, keepdims=True)
        out = jnp.where(lane == h, total, out)
    return out


def pick_halves(blocks, head_dim):
    lane = iota(blocks[0].shape, 1)
    per = LANES // head_dim
    out = []
    for first in range(0, len(blocks), per):
        block = blocks[first]
        for k in range(1, per):
            block = jnp.where(lane >= k * head_dim, blocks[first + k], block)
        out.append(block)
    return jnp.concatenate(out, 1)


def softplus(value):
    return jnp.maximum(value, 0.0) + jnp.log1p(jnp.exp(-jnp.abs(value)))


def running_sum(values, backward=False):
    rows = values.shape[0]
    row = iota(values.shape, 0)
    step = 1
    while step < rows:
        if backward:
            moved = jnp.where(row < rows - step, pltpu.roll(values, rows - step, 0), 0.0)
        else:
            moved = jnp.where(row >= step, pltpu.roll(values, step, 0), 0.0)
        values = values + moved
        step *= 2
    return values


def turn(values, cosine, sine, half):
    lane = iota(values.shape, 1)
    first = lax.rem(lane, 2 * half) < half
    swapped = jnp.where(
        first, pltpu.roll(values, LANES - half, 1), pltpu.roll(values, half, 1)
    )
    return values * cosine + swapped * sine


def decay_parts(step_pre, decay_log, bias):
    step = softplus(step_pre + bias)
    rate = -jnp.exp(decay_log)
    return step, rate, running_sum(step * rate)


def same_document(aux, row):
    span = aux.shape[0]
    same = aux[:, 5:6] == row
    causal = iota((span, span), 0) >= iota((span, span), 1)
    return jnp.where(jnp.logical_and(same, causal), 0.0, MASKED)


class Neighbours:
    def __init__(self, at):
        self.at = at

    def greet(self, flips=False):
        at = self.at
        barrier = pltpu.get_barrier_semaphore()
        end = at.devices - 1

        def signal(**where):
            pl.semaphore_signal(
                barrier, inc=1, device_id=where, device_id_type=pl.DeviceIdType.MESH
            )

        for other in (at.t_near, at.t_far, at.t_both):
            signal(tensor=other)
        signal(dp=at.pair)
        count = 4
        for step in (1, 2):
            low, high = at.dp >= step, at.dp + step <= end
            pl.when(low)(partial(signal, dp=at.dp - step))
            pl.when(high)(partial(signal, dp=at.dp + step))
            count = count + low.astype(jnp.int32) + high.astype(jnp.int32)
        if flips:
            for other in at.flips():
                signal(dp=other)
                count = count + 1
        pl.semaphore_wait(barrier, count)


class TensorTotal:
    def __init__(self, at, own, got, send, recv):
        self.at, self.own, self.got, self.send, self.recv = at, own, got, send, recv

    def copies(self):
        others = (self.at.t_near, self.at.t_far, self.at.t_both)
        return [
            remote(
                self.own, self.got.at[i], self.send.at[i], self.recv.at[i], {"tensor": other}
            )
            for i, other in enumerate(others)
        ]

    def start(self):
        for copy in self.copies():
            copy.start()

    def finish(self):
        for copy in self.copies():
            copy.wait()
        return self.own[...] + self.got[0] + self.got[1] + self.got[2]


class StatePass:
    def __init__(self, at, local, pair_in, chain_in, chain_out, share, result, sems, backward):
        self.at, self.local, self.pair_in = at, local, pair_in
        self.chain_in, self.chain_out, self.share, self.result = chain_in, chain_out, share, result
        self.backward = backward
        self.pair_send, self.pair_recv, self.chain_send, self.chain_recv = sems[:4]
        self.share_send, self.share_recv = sems[4:]
        self.half = local.shape[0] // 2
        self.size = result.shape[1]
        self.head = at.last if backward else at.first
        self.tail = at.first if backward else at.last
        self.onward = at.dp - 2 if backward else at.dp + 2

    def pair_copy(self):
        src = self.local.at[pl.ds((1 - self.at.p) * self.half, self.half)]
        return remote(
            src, self.pair_in, self.pair_send.at[0], self.pair_recv.at[0], {"dp": self.at.pair}
        )

    def chain_copy(self, i):
        return remote(
            self.chain_out.at[i],
            self.chain_in.at[i],
            self.chain_send.at[i],
            self.chain_recv.at[i],
            {"dp": self.onward},
        )

    def share_copy(self, i):
        return remote(
            self.share.at[i],
            self.result.at[self.at.p * self.half + i],
            self.share_send.at[i],
            self.share_recv.at[i],
            {"dp": self.at.pair},
        )

    def start(self):
        self.pair_copy().start()

    def run(self):
        at, size = self.at, self.size
        sooner = at.p == (1 if self.backward else 0)
        self.pair_copy().wait_recv()
        for i in range(self.half):
            mine = self.local[at.p * self.half + i].astype(F32)
            other = self.pair_in[i].astype(F32)
            one = jnp.where(sooner, mine, other)
            two = jnp.where(sooner, other, mine)
            state1, keep1 = one[:size], one[size : size + 1]
            state2, keep2 = two[:size], two[size : size + 1]

            @pl.when(self.head)
            def _():
                self.chain_in[i] = jnp.zeros(self.chain_in.shape[1:], BF16)

            @pl.when(jnp.logical_not(self.head))
            def _():
                self.chain_copy(i).wait_recv()

            before = self.chain_in[i].astype(F32)
            middle = keep1 * before + state1

            @pl.when(jnp.logical_not(self.tail))
            def _():
                self.chain_out[i] = (keep2 * middle + state2).astype(BF16)
                self.chain_copy(i).start()

            self.result[at.p * self.half + i] = jnp.where(sooner, before, middle).astype(BF16)
            self.share[i] = jnp.where(sooner, middle, before).astype(BF16)
            self.share_copy(i).start()

    def finish(self):
        at = self.at
        for i in range(self.half):
            remote(
                self.share.at[i],
                self.result.at[(1 - at.p) * self.half + i],
                self.share_send.at[i],
                self.share_recv.at[i],
                {"dp": at.pair},
            ).wait_recv()
            self.share_copy(i).wait_send()
            pl.when(jnp.logical_not(self.tail))(lambda: self.chain_copy(i).wait_send())
        self.pair_copy().wait_send()


def state_pass_scratch(half, size, width):
    dma = pltpu.SemaphoreType.DMA
    return [
        pltpu.VMEM((half, size + 16, width), BF16),
        pltpu.VMEM((half, size, width), BF16),
        pltpu.VMEM((half, size, width), BF16),
        pltpu.VMEM((half, size, width), BF16),
        dma((1,)),
        dma((1,)),
        dma((half,)),
        dma((half,)),
        dma((half,)),
        dma((half,)),
    ]


def packed_columns(layout, name):
    return pl.ds(*layout[name])


def span_row(rows, first, span):
    total = rows.shape[1]
    return pltpu.roll(rows, lax.rem(total - first, total), 1)[:, :span]


def shifted_column(row, before, back):
    span = row.shape[1]
    at, lane = iota((span, span), 0), iota((span, span), 1)
    now = jnp.where(lane == at - back, row, 0.0)
    earlier = jnp.where(lane == at - back + span, before, 0.0)
    return jnp.sum(now + earlier, 1, keepdims=True)


def mixer_kernel(cfg, *refs, joined=None):
    (
        x_ref, og_in, gain_ref, q_in, kv_in, mi_in, st_in, sp_in, gu_in, ao_in, mo_in, seg_ref,
        rope_any, xt_ref, xb_ref, stt_ref, sb_ref, head_ref, mgain_ref,
        w_all, nx, og, low, kv, q2, probs, att, ext, pre, step_buf, entering, carry, y_buf, z_buf,
        squares, aux_ref, seg_rows,
        local, xs_buf, nxh, rope_ref, rope_sem, row_send, row_recv, kv_sems, halo_sems, sq_own,
        sq_got, sq_send, sq_recv,
        *rest,
    ) = refs
    devices, layout, pieces, heads = (cfg[k] for k in ("devices", "layout", "pieces", "heads"))
    at = Place(devices)
    seqs, sub, width = x_ref.shape
    span = sub * 4
    tokens = seqs * span
    depth = q_in.shape[0]
    xw = layout["x"][1]
    head_dim = xw // heads
    sw = layout["state"][1]
    size = sw // 2
    mixed = xw + sw
    qw = layout["q"][1]
    at_dim = qw // 2
    count = devices * span
    pass_refs, sems = rest[:10], rest[10:]
    own_rows = pl.ds(pl.multiple_of(at.dp * depth, depth), depth)
    rope_copy = pltpu.make_async_copy(
        rope_any.at[pl.ds(pl.multiple_of(at.dp * span, span), span), :], rope_ref, rope_sem
    )
    rope_copy.start()
    kv[...] = jnp.zeros(kv.shape, BF16)

    def own(name, value):
        w_all[own_rows, packed_columns(layout, name)] = value

    own("x", mi_in[:, 1, :])
    own("state", st_in[...])
    own("step", jnp.zeros((depth, LANES), BF16))
    w_all[own_rows, pl.ds(layout["step"][0], sp_in.shape[1])] = sp_in[...]
    Neighbours(at).greet(flips=joined is not None)
    if joined is not None:
        own("down", joined.dn_in[...].T)
    gathers = []
    for i, (first, columns, cross) in enumerate(pieces):

        def view(block, first=first, columns=columns):
            return w_all.at[
                pl.ds(pl.multiple_of(block * depth, depth), depth), pl.ds(first, columns)
            ]

        kind = CrossGather if cross else LineGather
        gathers.append(kind(at, view, *sems[4 * i : 4 * i + 4]))

    def step(i, s):
        if s < at.lines - 1:
            gathers[i].step(s)
        if s == 2:
            pl.loop(3, max(at.lines - 1, 3))(lambda k: gathers[i].step(k))

    gathers[0].start()
    gain = gain_ref[...].reshape(1, width)
    mine = pl.ds(pl.multiple_of(at.t * sub, sub), sub)
    for s in range(seqs):
        nx[s, mine, :] = rms_rows(x_ref[s].astype(F32), gain).astype(BF16)
    half = seqs // 2

    def rows_of(buf):
        def view(rank, chunk):
            return buf.at[pl.ds(chunk * half, half), pl.ds(pl.multiple_of(rank * sub, sub), sub), :]

        return view

    row_nx = RowGather(at, rows_of(nx), row_send.at[0], row_recv.at[0])
    row_og = RowGather(at, rows_of(og), row_send.at[1], row_recv.at[1])
    for chunk in range(2):
        row_nx.start(chunk)
    own("kv", jnp.where(at.t < 2, kv_in[:, 0, :], kv_in[:, 1, :]))
    own("q", q_in[...])
    own("z", mi_in[:, 0, :])
    gathers[1].start()
    out_at, gu_at = layout["out"][0], layout["gu"][0]
    w_all[own_rows, pl.ds(out_at, qw)] = ao_in[...].T
    w_all[own_rows, pl.ds(out_at + qw, xw)] = mo_in[...].T
    ff = gu_in.shape[2]
    w_all[own_rows, pl.ds(gu_at, ff)] = gu_in[:, 0, :]
    w_all[own_rows, pl.ds(gu_at + ff, ff)] = gu_in[:, 1, :]
    for s in range(seqs):
        og[s, mine, :] = og_in[s]
    before, after = at.dp > 0, at.dp < devices - 1
    seg = seg_ref[...].astype(F32)
    now = span_row(seg, at.dp * span, span)
    old = jnp.where(before, span_row(seg, jnp.maximum(at.dp - 1, 0) * span, span), -1.0)
    seg_rows[...] = jnp.zeros(seg_rows.shape, F32)
    seg_rows[0:seqs, :] = now
    for s in range(seqs):
        row, earlier = now[s : s + 1, :], old[s : s + 1, :]
        column = to_column(row)
        same = [(shifted_column(row, earlier, k) == column).astype(F32) for k in (1, 2, 3)]
        same.append((column == earlier[:, span - 1 :]).astype(F32))
        same.append((column == row[:, span - 1 :]).astype(F32))
        same.append(column)
        lane = iota((span, LANES), 1)
        total = jnp.zeros((span, LANES), F32)
        for k, value in enumerate(same):
            total = jnp.where(lane == k, value, total)
        aux_ref[s] = total
    for chunk in range(2):
        row_nx.forward(chunk)
    for chunk in range(2):
        row_nx.finish(chunk)
    for chunk in range(2):
        row_og.start(chunk)

    def halo():
        return remote(
            nx.at[:, pl.ds(span - 16, 16), :],
            nxh,
            halo_sems.at[0],
            halo_sems.at[1],
            {"dp": at.dp + 1},
        )

    pl.when(after)(lambda: halo().start())
    step(0, 0)
    step(0, 1)
    step(1, 0)
    step(0, 2)
    gathers[2].start()
    step(1, 1)
    for chunk in range(2):
        row_og.forward(chunk)
    pl.when(before)(lambda: halo().wait_recv())

    @pl.when(jnp.logical_not(before))
    def _():
        nxh[...] = jnp.zeros(nxh.shape, BF16)

    gathers[0].finish()
    rows = nx[...].reshape(tokens, width)
    rows_before = nxh[...].reshape(seqs * 16, width)

    def project(name):
        return dot_nn(rows, w_all[:, packed_columns(layout, name)])

    for name, first in (("x", 0), ("state", xw)):
        columns = layout[name][1]
        value = project(name).astype(BF16).astype(F32)
        ext[:, pl.ds(8, span), pl.ds(first, columns)] = value.reshape(seqs, span, columns)
        value = dot_nn(rows_before, w_all[:, packed_columns(layout, name)])
        value = value.astype(BF16).astype(F32).reshape(seqs, 16, columns)
        ext[:, pl.ds(0, 8), pl.ds(first, columns)] = value[:, 8:, :]
    step_buf[...] = project("step").reshape(seqs, span, LANES)
    taps = jnp.concatenate([xt_ref[...], stt_ref[...]], 1)
    tap_bias = jnp.concatenate([xb_ref[...].reshape(1, xw), sb_ref[...].reshape(1, sw)], 1)
    step_bias, decay_log, skips = head_ref[0:1, :], head_ref[1:2, :], head_ref[2:3, :]

    def scan_parts(s):
        return decay_parts(step_buf[s], decay_log, step_bias)

    @pl.loop(0, seqs)
    def _(s):
        aux = aux_ref[s]
        total = tap_bias + taps[3:4, :] * ext[s, pl.ds(8, span), :]
        for back in (1, 2, 3):
            moved = ext[s, pl.ds(8 - back, span), :] * aux[:, back - 1 : back]
            total = total + taps[3 - back : 4 - back, :] * moved
        pre[s] = total
        active = total * jax.nn.sigmoid(total)
        step, _, running = scan_parts(s)
        scaled = active[:, :xw] * spread(step, heads, head_dim)
        xs_buf[s] = scaled.astype(BF16)
        end = running[span - 1 : span, :]
        tail = spread(jnp.exp(end - running) * aux[:, 4:5], heads, head_dim)
        state_in = active[:, xw : xw + size].astype(BF16)
        local[s, :size, :] = dot_tn(state_in, (scaled * tail).astype(BF16)).astype(BF16)
        keep = jnp.broadcast_to(jnp.exp(end) * aux[span - 1 : span, 3:4], (16, LANES))
        keep = spread(keep, heads, head_dim).astype(BF16)
        local[s, size : size + 16, :] = keep
        carry[s] = keep

    passing = StatePass(
        at, local, pass_refs[0], pass_refs[1], pass_refs[2], pass_refs[3], entering,
        pass_refs[4:], False,
    )
    passing.start()
    step(1, 2)
    gathers[1].finish()
    rope_copy.wait()
    lane = iota((span, LANES), 1)
    cosine, sine = rope_ref[:, :LANES], rope_ref[:, LANES:]
    pairs = project("kv").reshape(seqs, span, qw)
    key_cosine = jnp.where(lane < at_dim, cosine, 1.0)
    key_sine = jnp.where(lane < at_dim, sine, 0.0)
    scale = 1.0 / math.sqrt(at_dim)
    for s in range(seqs):
        kv[at.dp, s] = turn(pairs[s], key_cosine, key_sine, at_dim // 2).astype(BF16)
    kv_gather = LineGather(
        at,
        lambda block: kv.at[block],
        kv_sems.at[0],
        kv_sems.at[1],
        kv_sems.at[2],
        kv_sems.at[3],
        causal=True,
    )
    kv_gather.start()
    queries = project("q").reshape(seqs, span, qw)
    for s in range(seqs):
        turned = turn(queries[s], cosine, sine, at_dim // 2) * scale
        q2[s, :span, :] = jnp.where(lane < at_dim, turned, 0.0).astype(BF16)
        turned = pltpu.roll(turned, at_dim, 1)
        q2[s, span:, :] = jnp.where(lane < at_dim, turned, 0.0).astype(BF16)
    gathers[2].begin() if pieces[2][2] else None
    step(2, 0)
    passing.run()
    gathers[3].start()
    z_buf[...] = project("z").astype(BF16).reshape(seqs, span, xw)
    kv_gather.step(0)
    step(2, 1)
    @pl.loop(0, seqs)
    def _(s):
        aux = aux_ref[s]
        active = pre[s] * jax.nn.sigmoid(pre[s])
        _, _, running = scan_parts(s)
        running_rows = running.T
        allowed = same_document(aux, seg_rows[pl.ds(s, 1), :])
        state_in = active[:, xw : xw + size].astype(BF16)
        state_out = active[:, xw + size :].astype(BF16)
        joined = dot_nt(state_out, state_in)
        blocks = []
        for h in range(heads):
            gap = running[:, h : h + 1] - running_rows[h : h + 1, :]
            weight = (joined * jnp.exp(gap + allowed)).astype(BF16)
            cols = pl.ds(h * head_dim // LANES * LANES, LANES)
            blocks.append(dot_nn(weight, xs_buf[s, :, cols]))
        y_buf[s] = pick_halves(blocks, head_dim) + spread(skips, heads, head_dim) * active[:, :xw]

    pl.loop(1, at.lines - 1)(lambda s: kv_gather.step(s))
    step(2, 2)
    step(3, 0)
    passing.finish()
    sq_own[...] = jnp.zeros(sq_own.shape, F32)
    for s in range(seqs):
        aux = aux_ref[s]
        state_out = pre[s, :, pl.ds(xw + size, size)]
        state_out = (state_out * jax.nn.sigmoid(state_out)).astype(BF16)
        _, _, running = scan_parts(s)
        factor = spread(jnp.exp(running) * aux[:, 3:4], heads, head_dim)
        y = y_buf[s] + dot_nn(state_out, entering[s]) * factor
        y_buf[s] = y
        gate = z_buf[s].astype(F32)
        gated = y * gate * jax.nn.sigmoid(gate)
        sq_own[s : s + 1, :] = to_row(jnp.sum(gated * gated, 1, keepdims=True))
    total = TensorTotal(at, sq_own, sq_got, sq_send, sq_recv)
    total.start()
    kv_gather.finish()
    step(3, 1)
    if joined is not None:
        gathers[4].start()
    key_at = iota((span, count), 1)
    query_at = iota((span, count), 0) + at.dp * span
    causal = key_at <= query_at

    @pl.loop(0, seqs)
    def _(s):
        keys = kv[:, s].reshape(count, qw)
        row = seg_ref[pl.ds(s, 1), :].astype(F32)
        allowed = jnp.logical_and(aux_ref[s][:, 5:6] == row, causal)
        bias = jnp.where(allowed, 0.0, MASKED)
        outs = []
        for h in range(2):
            part = pl.ds(h * span, span)
            scores = dot_nt(q2[s, part, :], keys) + bias
            power = jnp.exp(scores - jnp.max(scores, 1, keepdims=True))
            weight = power * (1.0 / jnp.sum(power, 1, keepdims=True))
            weight = weight.astype(BF16)
            probs[s, part, :] = weight
            outs.append(dot_nn(weight, keys))
        att[s] = jnp.where(lane < at_dim, pltpu.roll(outs[0], at_dim, 1), outs[1])

    low[:, pl.ds(0, qw)] = att[...].reshape(tokens, qw).astype(BF16)
    squares[...] = total.finish()
    for s in range(seqs):
        gate = z_buf[s].astype(F32)
        gated = y_buf[s] * gate * jax.nn.sigmoid(gate)
        norm = lax.rsqrt(to_column(squares[s : s + 1, :]) / (4 * xw) + EPSILON)
        value = gated * norm * mgain_ref[...].reshape(1, xw)
        low[pl.ds(s * span, span), pl.ds(qw, xw)] = value.astype(BF16)
    for chunk in range(2):
        row_og.finish(chunk)
    def drain():
        for gather in [*gathers[:3], kv_gather]:
            gather.drain()
        for row in (row_nx, row_og):
            for chunk in range(2):
                row.drain(chunk)
        pl.when(after)(lambda: halo().wait_send())

    if joined is not None:
        gathers[2].finish()
        joined.step, joined.gathers = step, gathers
        joined.drains.append(drain)
        return
    step(3, 2)
    gathers[2].finish()
    gathers[3].finish()
    gathers[3].drain()
    drain()


def gather_sems(devices, pieces):
    dma = pltpu.SemaphoreType.DMA
    out = []
    for _, _, cross in pieces:
        out += [dma((devices,)) for _ in range(4)] if cross else line_gather_sems(devices)
    return out


def mixer_specs(cfg, columns):
    devices, layout, pieces, heads = (cfg[k] for k in ("devices", "layout", "pieces", "heads"))
    seqs, sub, width = cfg["rows"]
    span = sub * 4
    tokens = seqs * span
    xw, sw, qw = (layout[k][1] for k in ("x", "state", "q"))
    size = sw // 2
    count = devices * span
    dma = pltpu.SemaphoreType.DMA
    outs = (
        ((width, columns), BF16),
        ((seqs, span, width), BF16),
        ((seqs, span, width), BF16),
        ((tokens, qw + xw), BF16),
        ((devices, seqs, span, qw), BF16),
        ((seqs, 2 * span, qw), BF16),
        ((seqs, 2 * span, count), BF16),
        ((seqs, span, qw), F32),
        ((seqs, span + 8, xw + sw), F32),
        ((seqs, span, xw + sw), F32),
        ((seqs, span, LANES), F32),
        ((seqs, size, xw), BF16),
        ((seqs, 16, xw), BF16),
        ((seqs, span, xw), F32),
        ((seqs, span, xw), BF16),
        ((8, span), F32),
        ((seqs, span, LANES), F32),
        ((8, span), F32),
    )
    scratch = [
        pltpu.VMEM((seqs, size + 16, xw), BF16),
        pltpu.VMEM((seqs, span, xw), BF16),
        pltpu.VMEM((seqs, 16, width), BF16),
        pltpu.VMEM((span, 2 * LANES), F32),
        dma,
        dma((2, 2, 3)),
        dma((2, 2, 4)),
        dma((4, devices)),
        dma((2,)),
        pltpu.VMEM((8, span), F32),
        pltpu.VMEM((3, 8, span), F32),
        dma((3,)),
        dma((3,)),
    ]
    scratch += state_pass_scratch(seqs // 2, size, xw) + gather_sems(devices, pieces)
    return outs, scratch


def mixer(cfg, x, *args):
    outs, scratch = mixer_specs(cfg, cfg["layout"]["down"][0])
    vmem = pl.BlockSpec(memory_space=pltpu.VMEM)
    in_specs = [vmem] * (1 + len(args))
    in_specs[12] = pl.BlockSpec(memory_space=pl.ANY)
    return pl.pallas_call(
        partial(mixer_kernel, cfg),
        out_shape=tuple(jax.ShapeDtypeStruct(*out) for out in outs),
        in_specs=in_specs,
        out_specs=(vmem,) * len(outs),
        scratch_shapes=scratch,
        compiler_params=pltpu.CompilerParams(
            collective_id=0, has_side_effects=True, vmem_limit_bytes=VMEM_BYTES
        ),
        name="mixer",
    )(x, *args)


def back_kernel(cfg, *refs, joined=None):
    (
        x_ref, gh_ref, gain_ref, w_any, nx_ref, og_ref, gb_ref, low_ref, nf_any, dgu_any, act_ref,
        kv_any, q2_ref, probs_any, att_ref, ext_ref, pre_ref, step_ref, entering, carry, y_ref,
        z_ref, squares, aux_ref, seg_ref, rope_any, xt_ref, stt_ref, head_ref, mgain_ref, fgain_ref,
        rg_ref, dw_ref, sums, kvs,
        w_ref, d_in, dlow, dy, dbc, dcum, ext_grad, halo_got, local2, after_state, keys_buf,
        prob_buf, dkv, dkv_got, dkv_line, dkv_own,
        part, near, far, grads, got, line, line2, small_near, small_far, small_dp, kv_near, kv_far,
        sq_own, sq_got,
        rope_ref, w_sem, early_sems, rope_sem, load_sems, halo_sems, sq_send, sq_recv, send, recv, small_send, small_recv,
        dp_send, dp_recv, kv_send, kv_recv,
        *rest,
    ) = refs
    devices, layout, pieces, heads = (cfg[k] for k in ("devices", "layout", "scatters", "heads"))
    at = Place(devices)
    seqs, sub, width = x_ref.shape
    span = sub * 4
    tokens = seqs * span
    half = seqs // 2
    rows = half * span
    depth = width // devices
    xw, sw, qw = (layout[k][1] for k in ("x", "state", "q"))
    size = sw // 2
    head_dim = xw // heads
    at_dim = qw // 2
    mixed = xw + sw
    count = devices * span
    in_w = layout["in"][1]
    pass_refs, kv_sems, sems = rest[:10], rest[10:16], rest[16:]
    slots = 1 if joined is not None else keys_buf.shape[0]

    def loads(s):
        slot = s % slots
        return (
            pltpu.make_async_copy(kv_any.at[:, s], keys_buf.at[slot], load_sems.at[0, slot]),
            pltpu.make_async_copy(probs_any.at[s], prob_buf.at[slot], load_sems.at[1, slot]),
        )

    if joined is None:
        load = pltpu.make_async_copy(w_any.at[:, pl.ds(0, w_ref.shape[1])], w_ref, w_sem)
        load.start()
        early = (
            pltpu.make_async_copy(nf_any, part, early_sems.at[0]),
            pltpu.make_async_copy(dgu_any, d_in.at[:, pl.ds(0, dgu_any.shape[1])], early_sems.at[1]),
        )
        for copy in early:
            copy.start()
        rope_copy = pltpu.make_async_copy(
            rope_any.at[pl.ds(pl.multiple_of(at.dp * span, span), span), :], rope_ref, rope_sem
        )
        rope_copy.start()
        for copy in loads(0):
            copy.start()
        Neighbours(at).greet(flips=True)
        nf_ref, dgu_ref = part, d_in
    else:
        w_ref, nf_ref, dgu_ref = w_any, nf_any, dgu_any
    taps = jnp.concatenate([xt_ref[...], stt_ref[...]], 1)
    step_bias, decay_log, skips = head_ref[0:1, :], head_ref[1:2, :], head_ref[2:3, :]
    mixer_scale = mgain_ref[...].reshape(1, xw)

    def rows_of(buf):
        def view(rank, chunk):
            return buf.at[pl.ds(chunk * half, half), pl.ds(pl.multiple_of(rank * sub, sub), sub), :]

        return view

    scatters = []
    used = 0
    slots_used = 0
    kept = layout["gu"][0]

    def terms(first):
        return w_any if joined is not None and first >= kept else grads

    for first, columns, cross in pieces:

        def block(buf, k, first=first, columns=columns):
            return buf.at[pl.ds(pl.multiple_of(k * depth, depth), depth), pl.ds(first, columns)]

        if cross:
            wide = pl.ds(slots_used, columns)
            slots_used += columns
            scatters.append(
                CrossScatter(
                    at,
                    partial(block, terms(first)),
                    block(got, 0),
                    lambda zz, q, wide=wide: line2.at[
                        pl.ds(pl.multiple_of((zz * 2 + q) * depth, depth), depth), wide
                    ],
                    sems[used : used + 5],
                )
            )
            used += 5
        else:
            scatters.append(
                LineScatter(
                    at,
                    partial(block, terms(first)),
                    partial(block, got),
                    lambda zz, block=block: block(line, zz + 1),
                    partial(block, line),
                    sems[used : used + 6],
                )
            )
            used += 6

    def steps(i):
        @pl.loop(0, at.lines - 1)
        def _(s):
            scatters[i].step(s)

        if pieces[i][2]:
            scatters[i].join()

    def finish(i):
        first, columns, _ = pieces[i]
        scatters[i].finish(dw_ref.at[:, pl.ds(first, columns)])

    def product(lhs, rhs_ref, first, columns, into):
        tile = 2 * LANES if columns % (2 * LANES) == 0 else LANES

        @pl.loop(0, columns // tile)
        def _(j):
            src = pl.ds(pl.multiple_of(first + j * tile, LANES), tile)
            dst = pl.ds(pl.multiple_of(into + j * tile, LANES), tile)
            terms(into)[:, dst] = dot_tn(lhs, rhs_ref[:, src]).astype(BF16)

    def weights(i, lhs_ref, rhs_ref, first):
        into, columns, _ = pieces[i]
        product(lhs_ref[...].reshape(tokens, width), rhs_ref, first, columns, into)

    ff = layout["down"][1]

    def activations_ready():
        if joined is not None:
            joined.gathers[3].drain()
            joined.gathers[4].drain()
        weights(0, og_ref, act_ref, 0)
        scatters[0].start()

    if joined is not None:
        joined.activations_ready = activations_ready
        yield
    else:
        activations_ready()
        load.wait()
    dlow[...] = dot_nn(
        gb_ref[...].reshape(tokens, width), w_ref[:, pl.ds(*layout["out"])]
    )
    mixer_gain = jnp.zeros((1, xw), F32)
    sq_own[...] = jnp.zeros(sq_own.shape, F32)
    for s in range(seqs):
        gate = z_ref[s].astype(F32)
        gated = y_ref[s] * gate * jax.nn.sigmoid(gate)
        norm = lax.rsqrt(to_column(squares[s : s + 1, :]) / (4 * xw) + EPSILON)
        grad = dlow[pl.ds(s * span, span), pl.ds(qw, xw)]
        mixer_gain = mixer_gain + jnp.sum(grad * gated * norm, 0, keepdims=True)
        inner = jnp.sum(gated * grad * mixer_scale, 1, keepdims=True)
        sq_own[s : s + 1, :] = to_row(inner)
    total = TensorTotal(at, sq_own, sq_got, sq_send, sq_recv)
    total.start()
    if joined is None:
        for copy in early:
            copy.wait()
    weights(1, nf_ref, dgu_ref, 0)
    weights(2, nf_ref, dgu_ref, ff)
    inner_rows = total.finish()
    for s in range(seqs):
        gate = z_ref[s].astype(F32)
        sigmoid = jax.nn.sigmoid(gate)
        gated = y_ref[s] * gate * sigmoid
        norm = lax.rsqrt(to_column(squares[s : s + 1, :]) / (4 * xw) + EPSILON)
        inner = to_column(inner_rows[s : s + 1, :])
        term = dlow[pl.ds(s * span, span), pl.ds(qw, xw)] * mixer_scale
        grad = norm * (term - gated * (norm * norm * inner / (4 * xw)))
        dy[s] = grad * gate * sigmoid
        grad = grad * y_ref[s] * sigmoid * (1.0 + gate * (1.0 - sigmoid))
        d_in[pl.ds(s * span, span), pl.ds(*layout["z"])] = grad.astype(BF16)

    def parts(s):
        active = pre_ref[s] * jax.nn.sigmoid(pre_ref[s])
        step, rate, running = decay_parts(step_ref[s], decay_log, step_bias)
        state_in = active[:, xw : xw + size].astype(BF16)
        state_out = active[:, xw + size :].astype(BF16)
        return active[:, :xw], state_in, state_out, step, rate, running

    @pl.loop(0, seqs)
    def _(s):
        _, _, state_out, _, _, running = parts(s)
        factor = spread(jnp.exp(running) * aux_ref[s][:, 3:4], heads, head_dim)
        low = (dy[s] * factor).astype(BF16)
        local2[s, :size, :] = dot_tn(state_out, low).astype(BF16)
        local2[s, size:, :] = carry[s]

    passing = StatePass(
        at, local2, pass_refs[0], pass_refs[1], pass_refs[2], pass_refs[3], after_state,
        pass_refs[4:], True,
    )
    passing.start()
    scatters[1].start()
    weights(3, gb_ref, low_ref, 0)
    steps(0)
    @pl.loop(0, seqs)
    def _(s):
        x, state_in, state_out, step, _, running = parts(s)
        running_rows = running.T
        allowed = same_document(aux_ref[s], seg_ref[pl.ds(s, 1), :])
        xs = (x * spread(step, heads, head_dim)).astype(BF16)
        joined = dot_nt(state_out, state_in)
        lane = iota((span, LANES), 1)
        d_joined = jnp.zeros((span, span), F32)
        d_running = jnp.zeros((span, LANES), F32)
        blocks = []
        for h in range(heads):
            cols = slice(h * head_dim // LANES * LANES, h * head_dim // LANES * LANES + LANES)
            begin = h * head_dim % LANES
            inside = jnp.logical_and(lane >= begin, lane < begin + head_dim)
            grad = dy[s, :, pl.ds(cols.start, LANES)]
            decay = jnp.exp(running[:, h : h + 1] - running_rows[h : h + 1, :] + allowed)
            weight = joined * decay
            d_weight = dot_nt(jnp.where(inside, grad, 0.0).astype(BF16), xs[:, cols])
            d_joined = d_joined + d_weight * decay
            product_ = (d_weight * weight).astype(BF16)
            one = (lane == h).astype(BF16)
            d_running = d_running + dot_nn(product_, one) - dot_tn(product_, one)
            blocks.append(dot_tn(weight.astype(BF16), grad.astype(BF16)))
        dlow[pl.ds(pl.multiple_of(s * span, span), span), pl.ds(qw, xw)] = pick_halves(blocks, head_dim)
        d_joined = d_joined.astype(BF16)
        factor = spread(jnp.exp(running) * aux_ref[s][:, 3:4], heads, head_dim)
        crossed = dot_nn(state_out, entering[s]) * factor
        dcum[s] = d_running + head_sums(dy[s] * crossed, heads, head_dim)
        low = (dy[s] * factor).astype(BF16)
        dbc[s, :, :size] = dot_tn(d_joined, state_out)
        dbc[s, :, size:] = dot_nn(d_joined, state_in) + dot_nt(low, entering[s])

    passing.run()
    scatters[2].start()
    scatters[3].start()
    lane = iota((span, LANES), 1)
    upper = lane >= at_dim
    if joined is None:
        rope_copy.wait()
    cosine, sine = rope_ref[:, :LANES], rope_ref[:, LANES:]
    scale = 1.0 / math.sqrt(at_dim)
    for s in range(seqs):
        slot = s % slots
        if joined is None:
            for copy in loads(s):
                copy.wait()
            if slots > 1 and s + 1 < seqs:
                for copy in loads(s + 1):
                    copy.start()
            keys, weights_ref = keys_buf[slot].reshape(count, qw), prob_buf.at[slot]
        else:
            keys, weights_ref = kv_any[:, s].reshape(count, qw), probs_any.at[s]
        grad = dlow[pl.ds(s * span, span), pl.ds(0, qw)].astype(BF16).astype(F32)
        inner = grad * att_ref[s]
        d_keys = jnp.zeros((count, qw), F32)
        d_query = []
        for h in range(2):
            mine = upper if h else jnp.logical_not(upper)
            delta = jnp.sum(jnp.where(mine, inner, 0.0), 1, keepdims=True)
            moved = grad if h else pltpu.roll(grad, at_dim, 1)
            moved = jnp.where(upper, moved, 0.0).astype(BF16)
            weight = weights_ref[pl.ds(h * span, span), :]
            d_weight = dot_nt(moved, keys)
            d_score = (weight.astype(F32) * (d_weight - delta)).astype(BF16)
            query = q2_ref[s, pl.ds(h * span, span), :]
            d_keys = d_keys + dot_tn(d_score, query) + dot_tn(weight, moved)
            d_query.append(dot_nn(d_score, keys))
        dkv[:, s] = d_keys.astype(BF16).reshape(devices, span, qw)
        if joined is None and slots == 1 and s + 1 < seqs:
            for copy in loads(s + 1):
                copy.start()
        d_query = jnp.where(upper, pltpu.roll(d_query[1], at_dim, 1), d_query[0]) * scale
        d_in[pl.ds(s * span, span), pl.ds(*layout["q"])] = turn(
            d_query, cosine, -sine, at_dim // 2
        ).astype(BF16)
    kv_scatter = LineScatter(
        at,
        lambda k: dkv.at[k],
        lambda zz: dkv_got.at[zz],
        None,
        lambda zz: dkv_line.at[zz],
        kv_sems,
        causal=True,
    )
    kv_scatter.start()
    steps(1)
    finish(0)
    weights(4, nx_ref, d_in, pieces[4][0])
    scatters[4].start()
    passing.finish()
    tap_grads = [jnp.zeros((1, mixed), F32) for _ in range(4)]
    bias_grad = jnp.zeros((1, mixed), F32)
    step_grad = jnp.zeros((1, LANES), F32)
    decay_grad = jnp.zeros((1, LANES), F32)
    skip_grad = jnp.zeros((1, xw), F32)
    ext_grad[:, pl.ds(0, 8), :] = jnp.zeros((seqs, 8, mixed), F32)
    for s in range(seqs):
        aux = aux_ref[s]
        x, state_in, state_out, step, rate, running = parts(s)
        step_wide = spread(step, heads, head_dim)
        xs = x * step_wide
        end = running[span - 1 : span, :]
        tail = spread(jnp.exp(end - running) * aux[:, 4:5], heads, head_dim)
        later = after_state[s]
        found = dot_nn(state_in, later)
        weighted = xs * tail
        d_xs = dlow[pl.ds(s * span, span), pl.ds(qw, xw)] + found * tail
        d_in_state = dbc[s, :, :size] + dot_nt(weighted.astype(BF16), later)
        moved = head_sums(found * weighted, heads, head_dim)
        carried = jnp.sum(later.astype(F32) * entering[s].astype(F32), 0, keepdims=True)
        carried = head_sums(carried, heads, head_dim) * jnp.exp(end) * aux[span - 1 : span, 3:4]
        final = jnp.sum(moved, 0, keepdims=True) + carried
        d_running = dcum[s] - moved
        d_running = d_running + jnp.where(iota((span, LANES), 0) == span - 1, final, 0.0)
        d_decay = running_sum(d_running, backward=True)
        d_step = head_sums(d_xs * x, heads, head_dim) + d_decay * rate
        d_step = d_step * jax.nn.sigmoid(step_ref[s] + step_bias)
        d_in[pl.ds(s * span, span), pl.ds(*layout["step"])] = d_step.astype(BF16)
        step_grad = step_grad + jnp.sum(d_step, 0, keepdims=True)
        decay_grad = decay_grad + jnp.sum(d_decay * step, 0, keepdims=True) * rate
        skip_grad = skip_grad + jnp.sum(dy[s] * x, 0, keepdims=True)
        d_x = d_xs * step_wide + spread(skips, heads, head_dim) * dy[s]
        value = pre_ref[s]
        sigmoid = jax.nn.sigmoid(value)
        slope = sigmoid * (1.0 + value * (1.0 - sigmoid))
        outer = jnp.concatenate([d_x, d_in_state, dbc[s, :, size:]], 1) * slope
        bias_grad = bias_grad + jnp.sum(outer, 0, keepdims=True)
        ext_grad[s, pl.ds(8, span), :] = taps[3:4, :] * outer
        tap_grads[3] = tap_grads[3] + jnp.sum(
            outer * ext_ref[s, pl.ds(8, span), :], 0, keepdims=True
        )
        for back in (1, 2, 3):
            valid = outer * aux[:, back - 1 : back]
            tap_grads[3 - back] = tap_grads[3 - back] + jnp.sum(
                valid * ext_ref[s, pl.ds(8 - back, span), :], 0, keepdims=True
            )
            ext_grad[s, pl.ds(8 - back, span), :] += taps[3 - back : 4 - back, :] * valid
    before, after = at.dp > 0, at.dp < devices - 1

    def halo():
        return remote(
            ext_grad.at[:, pl.ds(0, 8), :],
            halo_got,
            halo_sems.at[0],
            halo_sems.at[1],
            {"dp": at.dp - 1},
        )

    pl.when(before)(lambda: halo().start())
    sums[...] = jnp.zeros(sums.shape, F32)
    sums[1:2, :] = fgain_ref[...]
    for k in range(4):
        sums[2 + k : 3 + k, pl.ds(0, sw)] = tap_grads[k][:, xw:]
        sums[8 + k : 9 + k, pl.ds(0, xw)] = tap_grads[k][:, :xw]
    sums[6:7, pl.ds(0, sw)] = bias_grad[:, xw:]
    sums[12:13, pl.ds(0, xw)] = bias_grad[:, :xw]
    sums[13:14, pl.ds(0, xw)] = mixer_gain
    sums[14:15, pl.ds(0, LANES)] = step_grad
    sums[14:15, pl.ds(LANES, LANES)] = decay_grad
    sums[14:15, pl.ds(2 * LANES, LANES)] = head_sums(
        jnp.broadcast_to(skip_grad, (8, xw)), heads, head_dim
    )[:1]
    steps(2)
    kv_scatter.run_causal(dkv_own)
    for s in range(seqs):
        key_cosine = jnp.where(upper, 1.0, cosine)
        key_sine = jnp.where(upper, 0.0, -sine)
        d_in[pl.ds(s * span, span), pl.ds(*layout["kv"])] = turn(
            dkv_own[s], key_cosine, key_sine, at_dim // 2
        ).astype(BF16)
    pl.when(after)(lambda: halo().wait_recv())
    ends = pl.ds(span, 8)

    @pl.when(after)
    def _():
        ext_grad[:, ends, :] += halo_got[...]

    value = ext_grad[:, pl.ds(8, span), :].reshape(tokens, mixed).astype(BF16)
    d_in[:, pl.ds(layout["x"][0], mixed)] = value
    back = RowScatter(
        at,
        rows_of(part),
        lambda which, chunk: near.at[which, pl.ds(chunk * half, half)],
        lambda chunk: far.at[pl.ds(chunk * half, half)],
        send,
        recv,
    )
    weights(5, nx_ref, d_in, pieces[5][0])
    scatters[5].start()
    back = RowScatter(
        at,
        rows_of(part),
        lambda which, chunk: near.at[which, pl.ds(chunk * half, half)],
        lambda chunk: far.at[pl.ds(chunk * half, half)],
        send,
        recv,
    )
    for c in range(2):
        value = dot_nt(d_in[pl.ds(c * rows, rows), :], w_ref[:, pl.ds(0, in_w)])
        part[pl.ds(c * half, half)] = value.astype(BF16).reshape(half, span, width)
        back.start(c)
    weights(6, nx_ref, d_in, pieces[6][0])
    scatters[6].start()
    steps(3)
    finish(1)
    for c in range(2):
        back.middle(c)
    steps(4)
    finish(2)
    total = jnp.zeros((1, width), F32)
    gain = gain_ref[...].reshape(1, width)
    for c in range(2):
        seq = pl.ds(c * half, half)
        grad, terms = rms_rows_grad(x_ref[seq].astype(F32), gain, back.finish(c))
        rg_ref[seq] = gh_ref[seq] + grad
        total = total + jnp.sum(terms.reshape(half * sub, width), 0, keepdims=True)
    sums[0:1, :] = total
    exchanges = [
        (sums.at[pl.ds(0, 8)], small_near, small_send.at[0], small_recv.at[0], {"tensor": at.t_near}),
        (sums.at[pl.ds(0, 8)], small_far, small_send.at[1], small_recv.at[1], {"tensor": at.t_far}),
    ] + [
        (sums, small_dp.at[i], dp_send.at[i], dp_recv.at[i], {"dp": other})
        for i, other in enumerate(at.flips())
    ]

    def begin(i):
        remote(*exchanges[i]).start()

    def end(i):
        remote(*exchanges[i]).wait()
        into, other = exchanges[i][:2]
        into[...] += other[...]

    begin(0)
    finish(3)
    end(0)
    begin(1)
    steps(5)
    end(1)
    begin(2)
    finish(4)
    end(2)
    begin(3)
    steps(6)
    end(3)
    finish(5)
    kvw = layout["kv"][1]
    kv_near[0, :, pl.ds(0, kvw)] = dw_ref[:, pl.ds(*layout["kv"])]
    kv_near[0, :, pl.ds(kvw, sw)] = dw_ref[:, pl.ds(*layout["state"])]
    copy = remote(kv_near.at[0], kv_near.at[1], kv_send.at[0], kv_recv.at[0], {"tensor": at.t_near})
    copy.start()
    begin(4)
    finish(6)
    copy.wait()
    kv_far[0] = kv_near[0] + kv_near[1]
    copy = remote(kv_far.at[0], kv_far.at[1], kv_send.at[1], kv_recv.at[1], {"tensor": at.t_far})
    copy.start()
    end(4)
    for i in range(5, len(exchanges)):
        begin(i)
        end(i)
    copy.wait()
    kvs[:, pl.ds(0, kvw)] = kv_far[0, :, pl.ds(0, kvw)]
    kvs[:, pl.ds(kvw, kvw)] = kv_far[1, :, pl.ds(0, kvw)]

    @pl.when(at.t >= 2)
    def _():
        kvs[:, pl.ds(0, kvw)] = kv_far[1, :, pl.ds(0, kvw)]
        kvs[:, pl.ds(kvw, kvw)] = kv_far[0, :, pl.ds(0, kvw)]

    kvs[:, pl.ds(2 * kvw, sw)] = kv_far[0, :, pl.ds(kvw, sw)] + kv_far[1, :, pl.ds(kvw, sw)]
    for scatter in [*scatters, kv_scatter]:
        scatter.drain()
    for c in range(2):
        back.drain(c)
    pl.when(before)(lambda: halo().wait_send())
    yield


def scatter_sems(devices, pieces):
    dma = pltpu.SemaphoreType.DMA
    out = []
    for _, _, cross in pieces:
        if cross:
            out += [dma((2,))] + [dma((devices,)) for _ in range(4)]
        else:
            out += line_scatter_sems(devices)
    return out


def back_specs(cfg, joined=False):
    devices, layout, pieces = (cfg[k] for k in ("devices", "layout", "scatters"))
    seqs, sub, width = cfg["rows"]
    span = sub * 4
    tokens = seqs * span
    half = seqs // 2
    depth = width // devices
    lines = devices // 2
    columns = layout["down"][0] + layout["down"][1]
    xw, sw, qw, kvw = (layout[k][1] for k in ("x", "state", "q", "kv"))
    size = sw // 2
    mixed = xw + sw
    in_w = layout["in"][1]
    own = (seqs, sub, width)
    rounds = devices.bit_length() - 1
    crossed = max(LANES, sum(piece[1] for piece in pieces if piece[2]))
    slots = 2 if devices * span <= 2048 else 1
    dma = pltpu.SemaphoreType.DMA
    outs = (
        (own, F32),
        ((depth, columns), F32),
        ((16, width), F32),
        ((depth, 2 * kvw + sw), F32),
    )
    scratch = {
        "w": pltpu.VMEM((width, in_w + qw + xw), BF16),
        "d_in": pltpu.VMEM((tokens, in_w), BF16),
        "dlow": pltpu.VMEM((tokens, qw + xw), F32),
        "dy": pltpu.VMEM((seqs, span, xw), F32),
        "dbc": pltpu.VMEM((seqs, span, sw), F32),
        "dcum": pltpu.VMEM((seqs, span, LANES), F32),
        "ext_grad": pltpu.VMEM((seqs, span + 8, mixed), F32),
        "halo_got": pltpu.VMEM((seqs, 8, mixed), F32),
        "local2": pltpu.VMEM((seqs, size + 16, xw), BF16),
        "after_state": pltpu.VMEM((seqs, size, xw), BF16),
        "keys_buf": pltpu.VMEM((slots, devices, span, qw), BF16),
        "prob_buf": pltpu.VMEM((slots, 2 * span, devices * span), BF16),
        "dkv": pltpu.VMEM((devices, seqs, span, qw), BF16),
        "dkv_got": pltpu.VMEM((lines, seqs, span, qw), BF16),
        "dkv_line": pltpu.VMEM((lines, seqs, span, qw), BF16),
        "dkv_own": pltpu.VMEM((seqs, span, qw), F32),
        "part": pltpu.VMEM((seqs, span, width), BF16),
        "near": pltpu.VMEM((2,) + own, BF16),
        "far": pltpu.VMEM(own, BF16),
        "grads": pltpu.VMEM((width, layout["gu"][0] if joined else columns), BF16),
        "got": pltpu.VMEM((lines * depth, columns), BF16),
        "line": pltpu.VMEM(((lines + 1) * depth, columns), BF16),
        "line2": pltpu.VMEM(((lines + 1) * 2 * depth, crossed), BF16),
        "small_near": pltpu.VMEM((8, width), F32),
        "small_far": pltpu.VMEM((8, width), F32),
        "small_dp": pltpu.VMEM((rounds, 16, width), F32),
        "kv_near": pltpu.VMEM((2, depth, kvw + sw), F32),
        "kv_far": pltpu.VMEM((2, depth, kvw + sw), F32),
        "sq_own": pltpu.VMEM((8, span), F32),
        "sq_got": pltpu.VMEM((3, 8, span), F32),
        "rope": pltpu.VMEM((span, 2 * LANES), F32),
        "w_sem": dma,
        "early_sems": dma((2,)),
        "rope_sem": dma,
        "load_sems": dma((2, 2)),
        "halo_sems": dma((2,)),
        "sq_send": dma((3,)),
        "sq_recv": dma((3,)),
        "send": dma((2, 3)),
        "recv": dma((2, 4)),
        "small_send": dma((2,)),
        "small_recv": dma((2,)),
        "dp_send": dma((rounds,)),
        "dp_recv": dma((rounds,)),
        "kv_send": dma((2,)),
        "kv_recv": dma((2,)),
    }
    rest = (
        state_pass_scratch(half, size, xw)
        + line_scatter_sems(devices)
        + scatter_sems(devices, pieces)
    )
    return outs, scratch, rest


APART = (
    "w", "keys_buf", "prob_buf", "part", "rope", "w_sem", "early_sems", "rope_sem", "load_sems",
)


def run_back(cfg, *refs):
    for _ in back_kernel(cfg, *refs):
        pass


def backward(cfg, x, *args):
    outs, scratch, rest = back_specs(cfg)
    vmem = pl.BlockSpec(memory_space=pltpu.VMEM)
    in_specs = [vmem] * (1 + len(args))
    for i in (3, 8, 9, 11, 13, 25):
        in_specs[i] = pl.BlockSpec(memory_space=pl.ANY)
    return pl.pallas_call(
        partial(run_back, cfg),
        out_shape=tuple(jax.ShapeDtypeStruct(*out) for out in outs),
        in_specs=in_specs,
        out_specs=(vmem,) * len(outs),
        scratch_shapes=list(scratch.values()) + rest,
        compiler_params=pltpu.CompilerParams(
            collective_id=2, has_side_effects=True, vmem_limit_bytes=VMEM_BYTES
        ),
        name="backward",
    )(x, *args)


class Joined:
    def __init__(self, dn_in):
        self.dn_in = dn_in
        self.drains = []


def joined_kernel(cfg, *refs):
    devices, layout = cfg["devices"], cfg["layout"]
    inputs, refs = refs[:21], refs[21:]
    dn_in, fgain_ref = inputs[19:]
    x_ref, og_in, gain_ref = inputs[:3]
    rope_any, xt_ref, _, stt_ref, _, head_ref, mgain_ref = inputs[12:19]
    inputs = inputs[:19]
    block_out, rg, dw, sums, kvs = refs[:5]
    refs = refs[5:]

    def take(count):
        nonlocal refs
        taken, refs = refs[:count], refs[count:]
        return taken

    mix_outs, mix_scratch = mixer_specs(cfg, layout["down"][0] + layout["down"][1])
    mixed = take(len(mix_outs))
    mixed_scratch = take(len(mix_scratch))
    ffn_outs, buffers, _, sems = ffn_specs(cfg)
    fed = (block_out, *take(len(ffn_outs) - 1))
    fed_scratch = (*take(len(buffers)), None, None, None, *take(len(sems)))
    _, scratch, rest = back_specs(cfg, True)
    names = [name for name in scratch if name not in APART]
    mine = dict(zip(names, take(len(names))))
    mine["part"] = fed_scratch[0]
    mine["rope"] = mixed_scratch[3]
    back_scratch = [mine.get(name) for name in scratch] + list(take(len(rest)))
    (
        w_all, nx, og, low, kv, q2, probs, att, ext, pre, step_buf, entering, carry, y_buf, z_buf,
        squares, aux_ref, seg_rows,
    ) = mixed
    _, gh, gb, nf, act, dgu, gain_part = fed
    joined = Joined(dn_in)
    later = back_kernel(
        cfg, x_ref, gh, gain_ref, w_all, nx, og, gb, low, nf, dgu, act, kv, q2, probs, att, ext, pre,
        step_buf, entering, carry, y_buf, z_buf, squares, aux_ref, seg_rows, rope_any, xt_ref, stt_ref,
        head_ref, mgain_ref, gain_part, rg, dw, sums, kvs, *back_scratch, joined=joined,
    )
    mixer_kernel(cfg, *inputs, *mixed, *mixed_scratch, joined=joined)
    next(later)
    ffn_kernel(
        devices, layout, x_ref, low, og, og_in, fgain_ref, w_all, None, *fed, *fed_scratch,
        joined=joined,
    )
    next(later)
    for drain in joined.drains:
        drain()


def joined_layer(cfg, *args):
    layout = cfg["layout"]
    mix_outs, mix_scratch = mixer_specs(cfg, layout["down"][0] + layout["down"][1])
    ffn_outs, buffers, _, sems = ffn_specs(cfg)
    outs, scratch, rest = back_specs(cfg, True)
    vmem = pl.BlockSpec(memory_space=pltpu.VMEM)
    in_specs = [vmem] * len(args)
    in_specs[12] = pl.BlockSpec(memory_space=pl.ANY)
    return pl.pallas_call(
        partial(joined_kernel, cfg),
        out_shape=tuple(jax.ShapeDtypeStruct(*out) for out in (ffn_outs[0], *outs)),
        in_specs=in_specs,
        out_specs=(vmem,) * 5,
        scratch_shapes=[pltpu.VMEM(*out) for out in mix_outs]
        + mix_scratch
        + [pltpu.VMEM(*out) for out in ffn_outs[1:]]
        + buffers
        + sems
        + [ref for name, ref in scratch.items() if name not in APART]
        + rest,
        compiler_params=pltpu.CompilerParams(
            collective_id=0, has_side_effects=True, vmem_limit_bytes=VMEM_BYTES
        ),
        name="layer",
    )(*args)


def unpack_kernel(layout, local, *refs):
    (
        dw, kvs, sums, rg, block,
        block_out, rg_out, gain1, gain2, wq, wkv, wao, wmi, wst, wsp, cw, cb, csw, csb, sbias,
        dlog, skip, mgain, wmo, wgu, wdn,
    ) = refs
    block_out[...] = block[...]
    rg_out[...] = rg[...]
    width = sums.shape[1]
    xw, sw = layout["x"][1], layout["state"][1]
    qw = layout["q"][1]
    ff = layout["down"][1]
    kvw = layout["kv"][1]

    def part(name):
        return dw[:, pl.ds(*layout[name])]

    gain1[...] = sums[0:1, :].reshape(width)
    gain2[...] = sums[1:2, :].reshape(width)
    wq[...] = part("q")
    wkv[:, 0, :] = kvs[:, :kvw]
    wkv[:, 1, :] = kvs[:, kvw : 2 * kvw]
    out = part("out")
    wao[...] = out[:, :qw].T
    wmo[...] = out[:, qw:].T
    wdn[...] = part("down").T
    wmi[:, 0, :] = part("z")
    wmi[:, 1, :] = part("x")
    wst[...] = kvs[:, 2 * kvw :]
    wsp[...] = part("step")[:, :local]
    gate_up = part("gu")
    wgu[:, 0, :] = gate_up[:, :ff]
    wgu[:, 1, :] = gate_up[:, ff:]
    cw[...] = sums[8:12, :xw]
    cb[...] = sums[12:13, :xw].reshape(xw)
    csw[...] = sums[2:6, :sw]
    csb[...] = sums[6:7, :sw].reshape(sw)
    sbias[...] = sums[14:15, :local].reshape(local)
    dlog[...] = sums[14:15, LANES : LANES + local].reshape(local)
    skip[...] = sums[14:15, 2 * LANES : 2 * LANES + local].reshape(local)
    mgain[...] = sums[13:14, :xw].reshape(xw)


def unpack(layout, local, dw, kvs, sums, rg, block):
    depth = dw.shape[0]
    width = sums.shape[1]
    xw, sw, qw, ff, kvw = (layout[k][1] for k in ("x", "state", "q", "down", "kv"))

    def shape(*dims):
        return jax.ShapeDtypeStruct(dims, F32)

    outs = (
        jax.ShapeDtypeStruct(block.shape, BF16),
        shape(*rg.shape),
        shape(width),
        shape(width),
        shape(depth, qw),
        shape(depth, 2, kvw),
        shape(qw, depth),
        shape(depth, 2, xw),
        shape(depth, sw),
        shape(depth, local),
        shape(4, xw),
        shape(xw),
        shape(4, sw),
        shape(sw),
        shape(local),
        shape(local),
        shape(local),
        shape(xw),
        shape(xw, depth),
        shape(depth, 2, ff),
        shape(ff, depth),
    )
    vmem = pl.BlockSpec(memory_space=pltpu.VMEM)
    return pl.pallas_call(
        partial(unpack_kernel, layout, local),
        out_shape=outs,
        in_specs=[vmem] * 5,
        out_specs=(vmem,) * len(outs),
        name="unpack",
    )(dw, kvs, sums, rg, block)


def rope_table(length, head_dim):
    half = head_dim // 2
    frequency = np.exp(-math.log(ROTARY_BASE) * 2.0 * np.arange(half) / head_dim)
    angle = np.arange(length)[:, None] * frequency[None, :]
    cosine, sine = np.cos(angle), np.sin(angle)
    copies = LANES // head_dim
    table = [cosine, cosine] * copies + [-sine, sine] * copies
    return np.concatenate(table, 1).astype(np.float32)


def body(
    resid_in,
    segment_ids,
    out_grad,
    input_gain,
    ffn_gain,
    query_weight,
    keyvalue_weight,
    attention_output_weight,
    mixer_input_weight,
    state_input_weight,
    step_weight,
    conv_mixer,
    conv_mixer_bias,
    conv_state,
    conv_state_bias,
    step_bias,
    decay_log,
    skip_gain,
    mixer_gain,
    mixer_output_weight,
    gate_up_weight,
    down_weight,
):
    shard_count = lax.axis_size("dp")
    head_dim = keyvalue_weight.shape[2] // 2
    query_width = query_weight.shape[1]
    mixer_local = step_weight.shape[1]
    mixer_width = conv_mixer.shape[1]
    state_width = state_input_weight.shape[1]
    ff = down_weight.shape[0]
    layout = {}
    columns = 0
    for name, size in (
        ("x", mixer_width),
        ("state", state_width),
        ("step", LANES),
        ("kv", 2 * head_dim),
        ("q", query_width),
        ("z", mixer_width),
        ("out", query_width + mixer_width),
        ("gu", 2 * ff),
        ("down", ff),
    ):
        layout[name] = (columns, size)
        columns += size
    layout["in"] = (0, layout["out"][0])
    kv_at, q_at, gu_at = (layout[k][0] for k in ("kv", "q", "gu"))
    config = {
        "devices": shard_count,
        "layout": layout,
        "heads": mixer_local,
        "rows": resid_in.shape,
        "pieces": (
            (0, kv_at, False),
            (kv_at, layout["out"][0] - kv_at, False),
            (*layout["out"], True),
            (*layout["gu"], False),
        ),
        "scatters": (
            (*layout["down"], False),
            (gu_at, ff, False),
            (gu_at + ff, ff, False),
            (*layout["out"], True),
            (q_at, layout["out"][0] - q_at, False),
            (layout["state"][0], q_at - layout["state"][0], False),
            (*layout["x"], False),
        ),
    }

    def lanes(array):
        return jnp.pad(array, (0, LANES - array.shape[0]))

    head_rows = jnp.stack([lanes(step_bias), lanes(decay_log), lanes(skip_gain)])
    rope = jnp.asarray(rope_table(segment_ids.shape[1], head_dim))
    raw = (
        resid_in,
        out_grad,
        input_gain,
        query_weight,
        keyvalue_weight,
        mixer_input_weight,
        state_input_weight,
        step_weight,
        gate_up_weight,
        attention_output_weight,
        mixer_output_weight,
        segment_ids,
        rope,
        conv_mixer,
        conv_mixer_bias,
        conv_state,
        conv_state_bias,
        head_rows,
        mixer_gain,
    )
    if segment_ids.size <= JOINED_TOKENS:
        config["pieces"] = (*config["pieces"], (*layout["down"], False))
        block_out, resid_grad, weight_grads, sums, replicated = joined_layer(
            config, *raw, down_weight, ffn_gain
        )
        return unpack(
            layout, mixer_local, weight_grads, replicated, sums, resid_grad, block_out
        )
    (
        w_all, span_normed_input, span_gradient, branch_low, keys, queries, probs, attention, ext,
        pre, step_pre, entering, state_decay, mixer_y, gate_z, squares, aux, seg_rows,
    ) = mixer(config, *raw)
    block_out, grad_hidden, grad_branch, span_feedforward, activated, grad_gate_up, ffn_gain_part = (
        feed_forward(
            config,
            resid_in,
            branch_low,
            span_gradient,
            out_grad,
            ffn_gain,
            w_all,
            down_weight,
        )
    )
    resid_grad, weight_grads, sums, replicated = backward(
        config,
        resid_in,
        grad_hidden,
        input_gain,
        w_all,
        span_normed_input,
        span_gradient,
        grad_branch,
        branch_low,
        span_feedforward,
        grad_gate_up,
        activated,
        keys,
        queries,
        probs,
        attention,
        ext,
        pre,
        step_pre,
        entering,
        state_decay,
        mixer_y,
        gate_z,
        squares,
        aux,
        seg_rows,
        rope,
        conv_mixer,
        conv_state,
        head_rows,
        mixer_gain,
        ffn_gain_part,
    )
    return unpack(layout, mixer_local, weight_grads, replicated, sums, resid_grad, block_out)


def solution(mesh):
    placed = (
        P(None, ("dp", "tensor"), None),
        P(),
        P(None, ("dp", "tensor"), None),
        P(),
        P(),
        P("dp", "tensor"),
        P("dp", None, None),
        P("tensor", "dp"),
        P("dp", None, "tensor"),
        P("dp", None),
        P("dp", "tensor"),
        P(None, "tensor"),
        P("tensor"),
        P(),
        P(),
        P("tensor"),
        P("tensor"),
        P("tensor"),
        P("tensor"),
        P("tensor", "dp"),
        P("dp", None, "tensor"),
        P("tensor", "dp"),
    )
    return jax.shard_map(
        body,
        mesh=mesh,
        in_specs=placed,
        out_specs=(
            P(None, ("dp", "tensor"), None),
            P(None, ("dp", "tensor"), None),
            P(),
            P(),
            P("dp", "tensor"),
            P("dp", None, None),
            P("tensor", "dp"),
            P("dp", None, "tensor"),
            P("dp", None),
            P("dp", "tensor"),
            P(None, "tensor"),
            P("tensor"),
            P(),
            P(),
            P("tensor"),
            P("tensor"),
            P("tensor"),
            P("tensor"),
            P("tensor", "dp"),
            P("dp", None, "tensor"),
            P("tensor", "dp"),
        ),
        check_vma=False,
    )
```

profile of v0, /device:TPU:0, one launch (start us, length us, event | category | flops | bytes accessed | tf_op | source)
XLA Modules:
  0.0 282.4 jit_solution(2683061352354231137)
XLA Ops:
  0.7 0.7 pad_bitcast_fusion.2
  1.3 0.7 pad_bitcast_fusion
  2.0 0.6 pad_maximum_fusion.refs_17_
  2.6 1.4 copy.44.refs_7_
  4.0 273.4 %layer.1 = (bf16[4,32,1024]{2,1,0:T(8,128)(2,1)}, f32[4,32,1024]{2,1,0:T(8,128)}, f32[128,3456]{1,0:T(8,128)}, f32[16,1024]{1,0:T(8,128)}, f32[128,512]{1,0:T(8,128)}) custom-call(bf16[4,32,1024]{2,1,0:T(8,128)(2,1)} %refs_0_.1, bf16[4,32,1024]{2,1,0:T(8,128)(2,1)} %refs_1_.1, f32[1024]{0:T(1024)} %refs_2_.1, bf16[128,128]{1,0:T(8,128)(2,1)} %refs_3_.1, ...), custom_call_target="tpu_custom_call" | custom-call | tf_op jit(solution)/shard_map/layer/pallas_call | solution.py:2059
  277.4 3.5 %unpack.1 = (bf16[4,32,1024]{2,1,0:T(8,128)(2,1)}, f32[4,32,1024]{2,1,0:T(8,128)}, f32[1024]{0:T(1024)}, f32[1024]{0:T(1024)}, f32[128,128]{1,0:T(8,128)}, /*ind...) custom-call(f32[128,3456]{1,0:T(8,128)} %get-tuple-element.26.refs_0, ...), custom_call_target="tpu_custom_call" | custom-call | tf_op jit(solution)/shard_map/unpack/pallas_call | solution.py:2153
  280.9 1.5 copy.45
where the time goes:
time: 283 us; the launch traced here: 282 us
  Pallas kernels  277 us (98%)
  local copies, waits for them, and re-layouts  4.25 us (2%)
    pallas_call x1, Pallas kernels, joined_layer(): pl.pallas_call(partial(joined_kernel, cfg), out_shape=tuple((jax.ShapeDty...  273 us

commit v1 on v0

--- a/solution.py
+++ b/solution.py
@@ -218,19 +218,11 @@
                 self.send_left(block).wait_send()
 
 
-class LineScatter:
-    def __init__(self, place, part, got, right, left, sems, causal=False):
-        self.at, self.part = place, part
-        self.got, self.right, self.left = got, right, left
+class DirectScatter:
+    def __init__(self, place, part, got, line, sems, causal=False):
+        self.at, self.part, self.got, self.line = place, part, got, line
+        self.pair_send, self.pair_recv, self.line_send, self.line_recv = sems
         self.causal = causal
-        (
-            self.pair_send,
-            self.pair_recv,
-            self.right_send,
-            self.right_recv,
-            self.left_send,
-            self.left_recv,
-        ) = sems
 
     def pair_copy(self, zz):
         src = self.part(zz * 2 + 1 - self.at.p)
@@ -238,100 +230,49 @@
             src, self.got(zz), self.pair_send.at[zz], self.pair_recv.at[zz], {"dp": self.at.pair}
         )
 
-    def right_copy(self, zz):
-        src = self.part(zz * 2 + self.at.p)
+    def line_copy(self, zz):
+        target = zz * 2 + self.at.p
         return remote(
-            src,
-            self.right(zz),
-            self.right_send.at[zz],
-            self.right_recv.at[zz],
-            {"dp": self.at.dp + 2},
+            self.part(target),
+            self.line(self.at.z),
+            self.line_send.at[zz],
+            self.line_recv.at[self.at.z],
+            {"dp": target},
         )
 
-    def left_copy(self, zz):
-        src = self.part(zz * 2 + self.at.p)
-        return remote(
-            src, self.left(zz), self.left_send.at[zz], self.left_recv.at[zz], {"dp": self.at.dp - 2}
-        )
+    def line_arrived(self, zz):
+        here = self.part(self.at.dp)
+        remote(
+            here, self.line(zz), self.line_send.at[zz], self.line_recv.at[zz], {"dp": self.at.pair}
+        ).wait_recv()
+
+    def target(self, i):
+        return i if self.causal else lax.rem(self.at.z + 1 + i, self.at.lines)
 
     def start(self):
-        at = self.at
-
-        @pl.loop(0, at.z + 1 if self.causal else at.lines)
+        @pl.loop(0, self.at.z + 1 if self.causal else self.at.lines)
         def _(i):
-            self.pair_copy(i if self.causal else at.lines - 1 - i).start()
-
-    def step(self, i):
-        at = self.at
-        high, low = at.lines - 1 - i, i
-        if self.causal:
-            self.step_low(low)
-            return
-
-        @pl.when(at.z < at.lines // 2)
-        def _():
-            self.step_high(high)
-            self.step_low(low)
-
-        @pl.when(at.z >= at.lines // 2)
-        def _():
-            self.step_low(low)
-            self.step_high(high)
-
-    def step_high(self, high):
-        at = self.at
-
-        @pl.when(high > at.z)
-        def _():
-            self.pair_copy(high).wait_recv()
-            ref = self.part(high * 2 + at.p)
-
-            @pl.when(at.first)
-            def _():
-                add_into(ref, self.got(high))
-
-            @pl.when(jnp.logical_not(at.first))
-            def _():
-                self.right_copy(high).wait_recv()
-                add_into(ref, self.got(high), self.right(high))
-
-            self.right_copy(high).start()
-
-    def step_low(self, low):
-        at = self.at
-
-        @pl.when(low < at.z)
-        def _():
-            self.pair_copy(low).wait_recv()
-            ref = self.part(low * 2 + at.p)
-
-            @pl.when(at.last)
-            def _():
-                add_into(ref, self.got(low))
-
-            @pl.when(jnp.logical_not(at.last))
-            def _():
-                self.left_copy(low).wait_recv()
-                add_into(ref, self.got(low), self.left(low))
-
-            self.left_copy(low).start()
+            self.pair_copy(self.target(i)).start()
+
+    def send(self):
+        @pl.loop(0, self.at.z if self.causal else self.at.lines - 1)
+        def _(i):
+            zz = self.target(i)
+            self.pair_copy(zz).wait_recv()
+            add_into(self.part(zz * 2 + self.at.p), self.got(zz))
+            self.line_copy(zz).start()
 
     def finish(self, out):
         at = self.at
         self.pair_copy(at.z).wait_recv()
         out[...] = self.part(at.dp)[...].astype(F32) + self.got(at.z)[...].astype(F32)
 
-        if not self.causal:
-
-            @pl.when(jnp.logical_not(at.first))
+        @pl.loop(at.z + 1 if self.causal else 0, at.lines)
+        def _(zz):
+            @pl.when(zz != at.z)
             def _():
-                self.right_copy(at.z).wait_recv()
-                out[...] += self.right(at.z)[...].astype(F32)
-
-        @pl.when(jnp.logical_not(at.last))
-        def _():
-            self.left_copy(at.z).wait_recv()
-            out[...] += self.left(at.z)[...].astype(F32)
+                self.line_arrived(zz)
+                out[...] += self.line(zz)[...].astype(F32)
 
     def drain(self):
         at = self.at
@@ -339,125 +280,7 @@
         @pl.loop(0, at.z + 1 if self.causal else at.lines)
         def _(zz):
             self.pair_copy(zz).wait_send()
-            if not self.causal:
-                pl.when(zz > at.z)(lambda: self.right_copy(zz).wait_send())
-            pl.when(zz < at.z)(lambda: self.left_copy(zz).wait_send())
-
-    def run_causal(self, out):
-        @pl.loop(0, self.at.lines - 1)
-        def _(s):
-            self.step(s)
-
-        self.finish(out)
-
-
-class CrossScatter:
-    def __init__(self, place, part, got, line, sems):
-        self.at, self.part, self.got, self.line = place, part, got, line
-        self.pair_send, self.pair_recv = sems[0].at[0], sems[0].at[1]
-        self.right_send, self.right_recv, self.left_send, self.left_recv = sems[1:]
-
-    def right_copy(self, zz, q):
-        block = zz * 2 + q
-        return remote(
-            self.part(block),
-            self.line(zz + 1, q),
-            self.right_send.at[block],
-            self.right_recv.at[block],
-            {"dp": self.at.dp + 2},
-        )
-
-    def left_copy(self, zz, q):
-        block = zz * 2 + q
-        return remote(
-            self.part(block),
-            self.line(zz, q),
-            self.left_send.at[block],
-            self.left_recv.at[block],
-            {"dp": self.at.dp - 2},
-        )
-
-    def pair_copy(self):
-        return remote(
-            self.part(self.at.pair), self.got, self.pair_send, self.pair_recv, {"dp": self.at.pair}
-        )
-
-    def start(self):
-        pass
-
-    def step(self, i):
-        at = self.at
-        high, low = at.lines - 1 - i, i
-
-        @pl.when(at.z < at.lines // 2)
-        def _():
-            self.step_high(high)
-            self.step_low(low)
-
-        @pl.when(at.z >= at.lines // 2)
-        def _():
-            self.step_low(low)
-            self.step_high(high)
-
-    def step_high(self, high):
-        at = self.at
-
-        @pl.when(high > at.z)
-        def _():
-            for q in (1 - at.p, at.p):
-
-                @pl.when(jnp.logical_not(at.first))
-                def _():
-                    self.right_copy(high, q).wait_recv()
-                    add_into(self.part(high * 2 + q), self.line(high + 1, q))
-
-                self.right_copy(high, q).start()
-
-    def step_low(self, low):
-        at = self.at
-
-        @pl.when(low < at.z)
-        def _():
-            for q in (1 - at.p, at.p):
-
-                @pl.when(jnp.logical_not(at.last))
-                def _():
-                    self.left_copy(low, q).wait_recv()
-                    add_into(self.part(low * 2 + q), self.line(low, q))
-
-                self.left_copy(low, q).start()
-
-    def join(self):
-        at = self.at
-        for q in (1 - at.p, at.p):
-            ref = self.part(at.z * 2 + q)
-
-            @pl.when(jnp.logical_not(at.first))
-            def _():
-                self.right_copy(at.z, q).wait_recv()
-                add_into(ref, self.line(at.z + 1, q))
-
-            @pl.when(jnp.logical_not(at.last))
-            def _():
-                self.left_copy(at.z, q).wait_recv()
-                add_into(ref, self.line(at.z, q))
-
-            if q is not at.p:
-                self.pair_copy().start()
-
-    def finish(self, out):
-        self.pair_copy().wait_recv()
-        out[...] = self.part(self.at.dp)[...].astype(F32) + self.got[...].astype(F32)
-
-    def drain(self):
-        at = self.at
-        self.pair_copy().wait_send()
-
-        @pl.loop(0, at.devices)
-        def _(block):
-            zz, q = lax.div(block, 2), lax.rem(block, 2)
-            pl.when(zz > at.z)(lambda: self.right_copy(zz, q).wait_send())
-            pl.when(zz < at.z)(lambda: self.left_copy(zz, q).wait_send())
+            pl.when(zz != at.z)(lambda: self.line_copy(zz).wait_send())
 
 
 class RowGather:
@@ -541,8 +364,8 @@
     return [dma((devices,)), dma((devices // 2,)), dma((devices // 2,)), dma((devices // 2,))]
 
 
-def line_scatter_sems(devices):
-    return [pltpu.SemaphoreType.DMA((devices // 2,)) for _ in range(6)]
+def scatter_sems(devices):
+    return [pltpu.SemaphoreType.DMA((devices // 2,)) for _ in range(4)]
 
 
 def rms_rows(values, gain):
@@ -617,8 +440,12 @@
         load.wait()
         gather_step = gather.step
     else:
-        joined.step(3, 2)
-        gather_step = partial(joined.step, 4)
+        joined.step(5, 1)
+
+        def gather_step(s):
+            joined.step(6, s)
+            if s == 0:
+                joined.step(5, 2)
     for c in range(2):
         value = dot_nt(a_ref[tok_rows(c), :], w_ref[:, out_w])
         part[seq_rows(c)] = value.astype(BF16).reshape(half, span, width)
@@ -634,8 +461,8 @@
     gather_step(1)
     if joined is not None:
         gather_step(2)
-        joined.gathers[3].finish()
-        joined.gathers[4].finish()
+        for late in joined.gathers[4:]:
+            late.finish()
     for c in range(2):
         row_nf.forward(c)
     if joined is None:
@@ -661,10 +488,15 @@
     for c in range(2):
         value = dot_nt(act[tok_rows(c), :], down())
         part2[seq_rows(c)] = value.astype(BF16).reshape(half, span, width)
-    if joined is not None:
-        joined.activations_ready()
+
+    def beside(i):
+        if joined is not None:
+            joined.beside_feed_forward[i]()
+
+    beside(0)
     for c in range(2):
         back.middle(c)
+    beside(1)
     total = jnp.zeros((1, width), F32)
     for c in range(2):
         grad_hidden, terms = rms_rows_grad(hid[seq_rows(c)], gain, back.finish(c))
@@ -675,12 +507,15 @@
         row_gb.start(c)
         ffn.start(c)
     gain_grad[...] = total
+    beside(2)
     for c in range(2):
         row_gb.forward(c)
         ffn.middle(c)
     for c in range(2):
+        row_gb.finish(c)
+    for c in range(2):
         out_ref[seq_rows(c)] = (hid[seq_rows(c)] + ffn.finish(c)).astype(BF16)
-        row_gb.finish(c)
+
     def drain():
         for c in range(2):
             row_nf.drain(c)
@@ -849,11 +684,13 @@
             signal(tensor=other)
         signal(dp=at.pair)
         count = 4
-        for step in (1, 2):
-            low, high = at.dp >= step, at.dp + step <= end
-            pl.when(low)(partial(signal, dp=at.dp - step))
-            pl.when(high)(partial(signal, dp=at.dp + step))
-            count = count + low.astype(jnp.int32) + high.astype(jnp.int32)
+        low, high = at.dp > 0, at.dp < end
+        pl.when(low)(lambda: signal(dp=at.dp - 1))
+        pl.when(high)(lambda: signal(dp=at.dp + 1))
+        count = count + low.astype(jnp.int32) + high.astype(jnp.int32)
+        for away in range(2, at.devices, 2):
+            signal(dp=lax.rem(at.dp + away, at.devices))
+            count = count + 1
         if flips:
             for other in at.flips():
                 signal(dp=other)
@@ -897,78 +734,94 @@
         self.tail = at.first if backward else at.last
         self.onward = at.dp - 2 if backward else at.dp + 2
 
-    def pair_copy(self):
-        src = self.local.at[pl.ds((1 - self.at.p) * self.half, self.half)]
+    def blocks(self):
+        return range(self.result.shape[2] // LANES)
+
+    def columns(self, block):
+        return pl.ds(block * LANES, LANES)
+
+    def pair_copy(self, block):
+        columns = self.columns(block)
         return remote(
-            src, self.pair_in, self.pair_send.at[0], self.pair_recv.at[0], {"dp": self.at.pair}
+            self.local.at[pl.ds((1 - self.at.p) * self.half, self.half), :, columns],
+            self.pair_in.at[:, :, columns],
+            self.pair_send.at[block],
+            self.pair_recv.at[block],
+            {"dp": self.at.pair},
         )
 
-    def chain_copy(self, i):
+    def chain_copy(self, i, block):
+        columns = self.columns(block)
         return remote(
-            self.chain_out.at[i],
-            self.chain_in.at[i],
-            self.chain_send.at[i],
-            self.chain_recv.at[i],
+            self.chain_out.at[i, :, columns],
+            self.chain_in.at[i, :, columns],
+            self.chain_send.at[i, block],
+            self.chain_recv.at[i, block],
             {"dp": self.onward},
         )
 
-    def share_copy(self, i):
+    def share_copy(self, i, block, from_other=False):
+        columns = self.columns(block)
+        sender = 1 - self.at.p if from_other else self.at.p
         return remote(
-            self.share.at[i],
-            self.result.at[self.at.p * self.half + i],
-            self.share_send.at[i],
-            self.share_recv.at[i],
+            self.share.at[i, :, columns],
+            self.result.at[sender * self.half + i, :, columns],
+            self.share_send.at[i, block],
+            self.share_recv.at[i, block],
             {"dp": self.at.pair},
         )
 
     def start(self):
-        self.pair_copy().start()
+        for block in self.blocks():
+            self.pair_copy(block).start()
 
     def run(self):
+        for block in self.blocks():
+            self.pair_copy(block).wait_recv()
+            for i in range(self.half):
+                self.pass_on(i, block)
+
+    def pass_on(self, i, block):
         at, size = self.at, self.size
+        columns = self.columns(block)
         sooner = at.p == (1 if self.backward else 0)
-        self.pair_copy().wait_recv()
-        for i in range(self.half):
-            mine = self.local[at.p * self.half + i].astype(F32)
-            other = self.pair_in[i].astype(F32)
-            one = jnp.where(sooner, mine, other)
-            two = jnp.where(sooner, other, mine)
-            state1, keep1 = one[:size], one[size : size + 1]
-            state2, keep2 = two[:size], two[size : size + 1]
-
-            @pl.when(self.head)
-            def _():
-                self.chain_in[i] = jnp.zeros(self.chain_in.shape[1:], BF16)
-
-            @pl.when(jnp.logical_not(self.head))
-            def _():
-                self.chain_copy(i).wait_recv()
-
-            before = self.chain_in[i].astype(F32)
-            middle = keep1 * before + state1
-
-            @pl.when(jnp.logical_not(self.tail))
-            def _():
-                self.chain_out[i] = (keep2 * middle + state2).astype(BF16)
-                self.chain_copy(i).start()
-
-            self.result[at.p * self.half + i] = jnp.where(sooner, before, middle).astype(BF16)
-            self.share[i] = jnp.where(sooner, middle, before).astype(BF16)
-            self.share_copy(i).start()
+        mine = self.local[at.p * self.half + i, :, columns].astype(F32)
+        other = self.pair_in[i, :, columns].astype(F32)
+        one = jnp.where(sooner, mine, other)
+        two = jnp.where(sooner, other, mine)
+        state1, keep1 = one[:size], one[size : size + 1]
+        state2, keep2 = two[:size], two[size : size + 1]
+
+        @pl.when(self.head)
+        def _():
+            self.chain_in[i, :, columns] = jnp.zeros((size, LANES), BF16)
+
+        @pl.when(jnp.logical_not(self.head))
+        def _():
+            self.chain_copy(i, block).wait_recv()
+
+        before = self.chain_in[i, :, columns].astype(F32)
+        middle = keep1 * before + state1
+
+        @pl.when(jnp.logical_not(self.tail))
+        def _():
+            self.chain_out[i, :, columns] = (keep2 * middle + state2).astype(BF16)
+            self.chain_copy(i, block).start()
+
+        result = jnp.where(sooner, before, middle).astype(BF16)
+        self.result[at.p * self.half + i, :, columns] = result
+        self.share[i, :, columns] = jnp.where(sooner, middle, before).astype(BF16)
+        self.share_copy(i, block).start()
 
     def finish(self):
-        at = self.at
-        for i in range(self.half):
-            remote(
-                self.share.at[i],
-                self.result.at[(1 - at.p) * self.half + i],
-                self.share_send.at[i],
-                self.share_recv.at[i],
-                {"dp": at.pair},
-            ).wait_recv()
-            self.share_copy(i).wait_send()
-            pl.when(jnp.logical_not(self.tail))(lambda: self.chain_copy(i).wait_send())
-        self.pair_copy().wait_send()
+        for block in self.blocks():
+            for i in range(self.half):
+                self.share_copy(i, block, from_other=True).wait_recv()
+                self.share_copy(i, block).wait_send()
+                pl.when(jnp.logical_not(self.tail))(
+                    lambda: self.chain_copy(i, block).wait_send()
+                )
+            self.pair_copy(block).wait_send()
 
 
 def state_pass_scratch(half, size, width):
@@ -978,12 +831,12 @@
         pltpu.VMEM((half, size, width), BF16),
         pltpu.VMEM((half, size, width), BF16),
         pltpu.VMEM((half, size, width), BF16),
-        dma((1,)),
-        dma((1,)),
-        dma((half,)),
-        dma((half,)),
-        dma((half,)),
-        dma((half,)),
+        dma((width // LANES,)),
+        dma((width // LANES,)),
+        dma((half, width // LANES)),
+        dma((half, width // LANES)),
+        dma((half, width // LANES)),
+        dma((half, width // LANES)),
     ]
 
 
@@ -1007,10 +860,10 @@
 def mixer_kernel(cfg, *refs, joined=None):
     (
         x_ref, og_in, gain_ref, q_in, kv_in, mi_in, st_in, sp_in, gu_in, ao_in, mo_in, seg_ref,
-        rope_any, xt_ref, xb_ref, stt_ref, sb_ref, head_ref, mgain_ref,
+        rope_any, xt_ref, xb_ref, stt_ref, sb_ref, sbias_ref, dlog_ref, skip_ref, mgain_ref,
         w_all, nx, og, low, kv, q2, probs, att, ext, pre, step_buf, entering, carry, y_buf, z_buf,
-        squares, aux_ref, seg_rows,
-        local, xs_buf, nxh, rope_ref, rope_sem, row_send, row_recv, kv_sems, halo_sems, sq_own,
+        squares, aux_ref, seg_rows, head_ref, nxh,
+        local, xs_buf, kvh, kvx, kvx_sems, rope_ref, rope_sem, row_send, row_recv, kv_sems, halo_sems, sq_own,
         sq_got, sq_send, sq_recv,
         *rest,
     ) = refs
@@ -1034,18 +887,26 @@
         rope_any.at[pl.ds(pl.multiple_of(at.dp * span, span), span), :], rope_ref, rope_sem
     )
     rope_copy.start()
-    kv[...] = jnp.zeros(kv.shape, BF16)
+    kvh[...] = jnp.zeros(kvh.shape, BF16)
 
     def own(name, value):
         w_all[own_rows, packed_columns(layout, name)] = value
 
+    even = lax.rem(at.t, 2) == 0
     own("x", mi_in[:, 1, :])
     own("state", st_in[...])
-    own("step", jnp.zeros((depth, LANES), BF16))
-    w_all[own_rows, pl.ds(layout["step"][0], sp_in.shape[1])] = sp_in[...]
+    value = jnp.where(at.t < 2, kv_in[:, 0, :], kv_in[:, 1, :]).astype(F32)
+    value = jnp.where(even, value, pltpu.roll(value, at_dim, 1))
+    turned = jnp.concatenate(
+        [sp_in[...].astype(F32), jnp.zeros((LANES - sp_in.shape[0], depth), F32)], 0
+    ).T
+    turned = pltpu.roll(turned, at_dim, 1)
+    value = jnp.where(iota(value.shape, 1) < at_dim, value, turned)
+    own("ks", value.astype(BF16))
+    head_ref[...] = jnp.zeros(head_ref.shape, F32)
+    for k, ref in enumerate((sbias_ref, dlog_ref, skip_ref)):
+        head_ref[k : k + 1, 0:heads] = ref[...].reshape(1, heads)
     Neighbours(at).greet(flips=joined is not None)
-    if joined is not None:
-        own("down", joined.dn_in[...].T)
     gathers = []
     for i, (first, columns, cross) in enumerate(pieces):
 
@@ -1058,16 +919,23 @@
         gathers.append(kind(at, view, *sems[4 * i : 4 * i + 4]))
 
     def step(i, s):
+        if i >= len(gathers):
+            return
+        if s == 0 and pieces[i][2]:
+            gathers[i].begin()
         if s < at.lines - 1:
             gathers[i].step(s)
         if s == 2:
             pl.loop(3, max(at.lines - 1, 3))(lambda k: gathers[i].step(k))
 
+    def begin(i):
+        if i < len(gathers):
+            gathers[i].start()
+
     gathers[0].start()
+    gathers[1].start()
     gain = gain_ref[...].reshape(1, width)
     mine = pl.ds(pl.multiple_of(at.t * sub, sub), sub)
-    for s in range(seqs):
-        nx[s, mine, :] = rms_rows(x_ref[s].astype(F32), gain).astype(BF16)
     half = seqs // 2
 
     def rows_of(buf):
@@ -1079,19 +947,12 @@
     row_nx = RowGather(at, rows_of(nx), row_send.at[0], row_recv.at[0])
     row_og = RowGather(at, rows_of(og), row_send.at[1], row_recv.at[1])
     for chunk in range(2):
+        for s in range(chunk * half, chunk * half + half):
+            nx[s, mine, :] = rms_rows(x_ref[s].astype(F32), gain).astype(BF16)
         row_nx.start(chunk)
-    own("kv", jnp.where(at.t < 2, kv_in[:, 0, :], kv_in[:, 1, :]))
     own("q", q_in[...])
     own("z", mi_in[:, 0, :])
-    gathers[1].start()
-    out_at, gu_at = layout["out"][0], layout["gu"][0]
-    w_all[own_rows, pl.ds(out_at, qw)] = ao_in[...].T
-    w_all[own_rows, pl.ds(out_at + qw, xw)] = mo_in[...].T
-    ff = gu_in.shape[2]
-    w_all[own_rows, pl.ds(gu_at, ff)] = gu_in[:, 0, :]
-    w_all[own_rows, pl.ds(gu_at + ff, ff)] = gu_in[:, 1, :]
-    for s in range(seqs):
-        og[s, mine, :] = og_in[s]
+    begin(2)
     before, after = at.dp > 0, at.dp < devices - 1
     seg = seg_ref[...].astype(F32)
     now = span_row(seg, at.dp * span, span)
@@ -1114,8 +975,6 @@
         row_nx.forward(chunk)
     for chunk in range(2):
         row_nx.finish(chunk)
-    for chunk in range(2):
-        row_og.start(chunk)
 
     def halo():
         return remote(
@@ -1128,13 +987,23 @@
 
     pl.when(after)(lambda: halo().start())
     step(0, 0)
+    step(1, 0)
+    for s in range(seqs):
+        og[s, mine, :] = og_in[s]
+    for chunk in range(2):
+        row_og.start(chunk)
+    out_at, gu_at = layout["out"][0], layout["gu"][0]
+    w_all[own_rows, pl.ds(out_at, qw)] = ao_in[...].T
+    w_all[own_rows, pl.ds(out_at + qw, xw)] = mo_in[...].T
+    ff = gu_in.shape[2]
+    w_all[own_rows, pl.ds(gu_at, ff)] = gu_in[:, 0, :]
+    w_all[own_rows, pl.ds(gu_at + ff, ff)] = gu_in[:, 1, :]
+    if joined is not None:
+        own("down", joined.dn_in[...].T)
     step(0, 1)
-    step(1, 0)
+    step(1, 1)
     step(0, 2)
-    gathers[2].start()
-    step(1, 1)
-    for chunk in range(2):
-        row_og.forward(chunk)
+    step(1, 2)
     pl.when(before)(lambda: halo().wait_recv())
 
     @pl.when(jnp.logical_not(before))
@@ -1148,14 +1017,41 @@
     def project(name):
         return dot_nn(rows, w_all[:, packed_columns(layout, name)])
 
-    for name, first in (("x", 0), ("state", xw)):
+    def project_ext(name, first):
         columns = layout[name][1]
         value = project(name).astype(BF16).astype(F32)
         ext[:, pl.ds(8, span), pl.ds(first, columns)] = value.reshape(seqs, span, columns)
         value = dot_nn(rows_before, w_all[:, packed_columns(layout, name)])
         value = value.astype(BF16).astype(F32).reshape(seqs, 16, columns)
         ext[:, pl.ds(0, 8), pl.ds(first, columns)] = value[:, 8:, :]
-    step_buf[...] = project("step").reshape(seqs, span, LANES)
+
+    lane = iota((span, LANES), 1)
+    key_or_step = project("ks").reshape(seqs, span, LANES)
+    for s in range(seqs):
+        step_buf[s] = jnp.where(lane < at_dim, pltpu.roll(key_or_step[s], at_dim, 1), 0.0)
+    rope_copy.wait()
+    cosine, sine = rope_ref[:, :LANES], rope_ref[:, LANES:]
+    halves = []
+    for s in range(seqs):
+        turned = turn(key_or_step[s], cosine, sine, at_dim // 2)
+        halves.append(jnp.where(even, turned, key_or_step[s]))
+    for s in range(half):
+        pair = jnp.where(lane < at_dim, halves[s], pltpu.roll(halves[s + half], at_dim, 1))
+        kvh[at.dp, s] = pair.astype(BF16)
+    kv_gather = LineGather(
+        at,
+        lambda block: kvh.at[block],
+        kv_sems.at[0],
+        kv_sems.at[1],
+        kv_sems.at[2],
+        kv_sems.at[3],
+        causal=True,
+    )
+    kv_gather.start()
+    project_ext("state", xw)
+    step(2, 0)
+    gathers[1].finish()
+    project_ext("x", 0)
     taps = jnp.concatenate([xt_ref[...], stt_ref[...]], 1)
     tap_bias = jnp.concatenate([xb_ref[...].reshape(1, xw), sb_ref[...].reshape(1, sw)], 1)
     step_bias, decay_log, skips = head_ref[0:1, :], head_ref[1:2, :], head_ref[2:3, :]
@@ -1163,8 +1059,7 @@
     def scan_parts(s):
         return decay_parts(step_buf[s], decay_log, step_bias)
 
-    @pl.loop(0, seqs)
-    def _(s):
+    def convolve(s):
         aux = aux_ref[s]
         total = tap_bias + taps[3:4, :] * ext[s, pl.ds(8, span), :]
         for back in (1, 2, 3):
@@ -1188,41 +1083,29 @@
         at, local, pass_refs[0], pass_refs[1], pass_refs[2], pass_refs[3], entering,
         pass_refs[4:], False,
     )
+    pl.loop(0, half)(lambda i: convolve((1 - at.p) * half + i))
     passing.start()
-    step(1, 2)
-    gathers[1].finish()
-    rope_copy.wait()
-    lane = iota((span, LANES), 1)
-    cosine, sine = rope_ref[:, :LANES], rope_ref[:, LANES:]
-    pairs = project("kv").reshape(seqs, span, qw)
-    key_cosine = jnp.where(lane < at_dim, cosine, 1.0)
-    key_sine = jnp.where(lane < at_dim, sine, 0.0)
+    pl.loop(0, half)(lambda i: convolve(at.p * half + i))
+    kv_gather.step(0)
+    step(2, 1)
+    pl.loop(1, at.lines - 1)(lambda s: kv_gather.step(s))
+    passing.run()
+    begin(3)
+    step(2, 2)
+    gathers[2].finish()
     scale = 1.0 / math.sqrt(at_dim)
-    for s in range(seqs):
-        kv[at.dp, s] = turn(pairs[s], key_cosine, key_sine, at_dim // 2).astype(BF16)
-    kv_gather = LineGather(
-        at,
-        lambda block: kv.at[block],
-        kv_sems.at[0],
-        kv_sems.at[1],
-        kv_sems.at[2],
-        kv_sems.at[3],
-        causal=True,
-    )
-    kv_gather.start()
     queries = project("q").reshape(seqs, span, qw)
     for s in range(seqs):
         turned = turn(queries[s], cosine, sine, at_dim // 2) * scale
         q2[s, :span, :] = jnp.where(lane < at_dim, turned, 0.0).astype(BF16)
         turned = pltpu.roll(turned, at_dim, 1)
         q2[s, span:, :] = jnp.where(lane < at_dim, turned, 0.0).astype(BF16)
-    gathers[2].begin() if pieces[2][2] else None
-    step(2, 0)
-    passing.run()
-    gathers[3].start()
     z_buf[...] = project("z").astype(BF16).reshape(seqs, span, xw)
-    kv_gather.step(0)
-    step(2, 1)
+    kv_gather.finish()
+    kv_swap = remote(kvh, kvx, kvx_sems.at[0], kvx_sems.at[1], {"tensor": at.t_near})
+    kv_swap.start()
+    step(3, 0)
+    begin(4)
     @pl.loop(0, seqs)
     def _(s):
         aux = aux_ref[s]
@@ -1232,37 +1115,24 @@
         allowed = same_document(aux, seg_rows[pl.ds(s, 1), :])
         state_in = active[:, xw : xw + size].astype(BF16)
         state_out = active[:, xw + size :].astype(BF16)
-        joined = dot_nt(state_out, state_in)
+        joined_ = dot_nt(state_out, state_in)
         blocks = []
         for h in range(heads):
             gap = running[:, h : h + 1] - running_rows[h : h + 1, :]
-            weight = (joined * jnp.exp(gap + allowed)).astype(BF16)
+            weight = (joined_ * jnp.exp(gap + allowed)).astype(BF16)
             cols = pl.ds(h * head_dim // LANES * LANES, LANES)
             blocks.append(dot_nn(weight, xs_buf[s, :, cols]))
         y_buf[s] = pick_halves(blocks, head_dim) + spread(skips, heads, head_dim) * active[:, :xw]
 
-    pl.loop(1, at.lines - 1)(lambda s: kv_gather.step(s))
-    step(2, 2)
-    step(3, 0)
-    passing.finish()
-    sq_own[...] = jnp.zeros(sq_own.shape, F32)
-    for s in range(seqs):
-        aux = aux_ref[s]
-        state_out = pre[s, :, pl.ds(xw + size, size)]
-        state_out = (state_out * jax.nn.sigmoid(state_out)).astype(BF16)
-        _, _, running = scan_parts(s)
-        factor = spread(jnp.exp(running) * aux[:, 3:4], heads, head_dim)
-        y = y_buf[s] + dot_nn(state_out, entering[s]) * factor
-        y_buf[s] = y
-        gate = z_buf[s].astype(F32)
-        gated = y * gate * jax.nn.sigmoid(gate)
-        sq_own[s : s + 1, :] = to_row(jnp.sum(gated * gated, 1, keepdims=True))
-    total = TensorTotal(at, sq_own, sq_got, sq_send, sq_recv)
-    total.start()
-    kv_gather.finish()
     step(3, 1)
-    if joined is not None:
-        gathers[4].start()
+    step(4, 0)
+    kv_swap.wait()
+    wide = iota((devices, span, qw), 2) < at_dim
+    for s in range(half):
+        here, there = kvh[:, s].astype(F32), kvx[:, s].astype(F32)
+        keys, values = jnp.where(even, here, there), jnp.where(even, there, here)
+        kv[:, s] = jnp.where(wide, keys, pltpu.roll(values, at_dim, 2)).astype(BF16)
+        kv[:, s + half] = jnp.where(wide, pltpu.roll(keys, at_dim, 2), values).astype(BF16)
     key_at = iota((span, count), 1)
     query_at = iota((span, count), 0) + at.dp * span
     causal = key_at <= query_at
@@ -1285,6 +1155,29 @@
         att[s] = jnp.where(lane < at_dim, pltpu.roll(outs[0], at_dim, 1), outs[1])
 
     low[:, pl.ds(0, qw)] = att[...].reshape(tokens, qw).astype(BF16)
+    for chunk in range(2):
+        row_og.forward(chunk)
+    step(3, 2)
+    step(4, 1)
+    begin(5)
+    passing.finish()
+    sq_own[...] = jnp.zeros(sq_own.shape, F32)
+    for s in range(seqs):
+        aux = aux_ref[s]
+        state_out = pre[s, :, pl.ds(xw + size, size)]
+        state_out = (state_out * jax.nn.sigmoid(state_out)).astype(BF16)
+        _, _, running = scan_parts(s)
+        factor = spread(jnp.exp(running) * aux[:, 3:4], heads, head_dim)
+        y = y_buf[s] + dot_nn(state_out, entering[s]) * factor
+        y_buf[s] = y
+        gate = z_buf[s].astype(F32)
+        gated = y * gate * jax.nn.sigmoid(gate)
+        sq_own[s : s + 1, :] = to_row(jnp.sum(gated * gated, 1, keepdims=True))
+    total = TensorTotal(at, sq_own, sq_got, sq_send, sq_recv)
+    total.start()
+    step(4, 2)
+    step(5, 0)
+    begin(6)
     squares[...] = total.finish()
     for s in range(seqs):
         gate = z_buf[s].astype(F32)
@@ -1295,22 +1188,24 @@
     for chunk in range(2):
         row_og.finish(chunk)
     def drain():
-        for gather in [*gathers[:3], kv_gather]:
+        for gather in [*gathers[:4], kv_gather]:
             gather.drain()
         for row in (row_nx, row_og):
             for chunk in range(2):
                 row.drain(chunk)
         pl.when(after)(lambda: halo().wait_send())
 
+    gathers[3].finish()
     if joined is not None:
-        gathers[2].finish()
         joined.step, joined.gathers = step, gathers
         joined.drains.append(drain)
         return
-    step(3, 2)
-    gathers[2].finish()
-    gathers[3].finish()
-    gathers[3].drain()
+    step(5, 1)
+    step(5, 2)
+    for gather in gathers[4:]:
+        gather.finish()
+    for gather in gathers[4:]:
+        gather.drain()
     drain()
 
 
@@ -1350,11 +1245,15 @@
         ((8, span), F32),
         ((seqs, span, LANES), F32),
         ((8, span), F32),
+        ((8, LANES), F32),
+        ((seqs, 16, width), BF16),
     )
     scratch = [
         pltpu.VMEM((seqs, size + 16, xw), BF16),
         pltpu.VMEM((seqs, span, xw), BF16),
-        pltpu.VMEM((seqs, 16, width), BF16),
+        pltpu.VMEM((devices, seqs // 2, span, qw), BF16),
+        pltpu.VMEM((devices, seqs // 2, span, qw), BF16),
+        dma((2,)),
         pltpu.VMEM((span, 2 * LANES), F32),
         dma,
         dma((2, 2, 3)),
@@ -1392,12 +1291,12 @@
     (
         x_ref, gh_ref, gain_ref, w_any, nx_ref, og_ref, gb_ref, low_ref, nf_any, dgu_any, act_ref,
         kv_any, q2_ref, probs_any, att_ref, ext_ref, pre_ref, step_ref, entering, carry, y_ref,
-        z_ref, squares, aux_ref, seg_ref, rope_any, xt_ref, stt_ref, head_ref, mgain_ref, fgain_ref,
+        z_ref, squares, aux_ref, seg_ref, head_ref, nxh_ref, rope_any, xt_ref, stt_ref, mgain_ref, fgain_ref,
         rg_ref, dw_ref, sums, kvs,
         w_ref, d_in, dlow, dy, dbc, dcum, ext_grad, halo_got, local2, after_state, keys_buf,
-        prob_buf, dkv, dkv_got, dkv_line, dkv_own,
-        part, near, far, grads, got, line, line2, small_near, small_far, small_dp, kv_near, kv_far,
-        sq_own, sq_got,
+        prob_buf, dkv, dkv_other, dkv_swap, dkv_got, dkv_line, dkv_own,
+        part, near, far, grads, got, line, small_near, small_far, small_dp, kv_near, kv_far,
+        sq_own, sq_got, swap_sems,
         rope_ref, w_sem, early_sems, rope_sem, load_sems, halo_sems, sq_send, sq_recv, send, recv, small_send, small_recv,
         dp_send, dp_recv, kv_send, kv_recv,
         *rest,
@@ -1417,7 +1316,7 @@
     mixed = xw + sw
     count = devices * span
     in_w = layout["in"][1]
-    pass_refs, kv_sems, sems = rest[:10], rest[10:16], rest[16:]
+    pass_refs, kv_sems, sems = rest[:10], rest[10:14], rest[14:]
     slots = 1 if joined is not None else keys_buf.shape[0]
 
     def loads(s):
@@ -1457,56 +1356,28 @@
         return view
 
     scatters = []
-    used = 0
-    slots_used = 0
     kept = layout["gu"][0]
 
     def terms(first):
         return w_any if joined is not None and first >= kept else grads
 
-    for first, columns, cross in pieces:
+    for i, (first, columns) in enumerate(pieces):
 
         def block(buf, k, first=first, columns=columns):
             return buf.at[pl.ds(pl.multiple_of(k * depth, depth), depth), pl.ds(first, columns)]
 
-        if cross:
-            wide = pl.ds(slots_used, columns)
-            slots_used += columns
-            scatters.append(
-                CrossScatter(
-                    at,
-                    partial(block, terms(first)),
-                    block(got, 0),
-                    lambda zz, q, wide=wide: line2.at[
-                        pl.ds(pl.multiple_of((zz * 2 + q) * depth, depth), depth), wide
-                    ],
-                    sems[used : used + 5],
-                )
+        scatters.append(
+            DirectScatter(
+                at,
+                partial(block, terms(first)),
+                partial(block, got),
+                partial(block, line),
+                sems[4 * i : 4 * i + 4],
             )
-            used += 5
-        else:
-            scatters.append(
-                LineScatter(
-                    at,
-                    partial(block, terms(first)),
-                    partial(block, got),
-                    lambda zz, block=block: block(line, zz + 1),
-                    partial(block, line),
-                    sems[used : used + 6],
-                )
-            )
-            used += 6
-
-    def steps(i):
-        @pl.loop(0, at.lines - 1)
-        def _(s):
-            scatters[i].step(s)
-
-        if pieces[i][2]:
-            scatters[i].join()
+        )
 
     def finish(i):
-        first, columns, _ = pieces[i]
+        first, columns = pieces[i]
         scatters[i].finish(dw_ref.at[:, pl.ds(first, columns)])
 
     def product(lhs, rhs_ref, first, columns, into):
@@ -1519,23 +1390,33 @@
             terms(into)[:, dst] = dot_tn(lhs, rhs_ref[:, src]).astype(BF16)
 
     def weights(i, lhs_ref, rhs_ref, first):
-        into, columns, _ = pieces[i]
+        into, columns = pieces[i]
         product(lhs_ref[...].reshape(tokens, width), rhs_ref, first, columns, into)
 
     ff = layout["down"][1]
 
-    def activations_ready():
+    def gradients(i, *args):
+        weights(i, *args)
+        scatters[i].start()
+
+    def first():
         if joined is not None:
-            joined.gathers[3].drain()
-            joined.gathers[4].drain()
-        weights(0, og_ref, act_ref, 0)
-        scatters[0].start()
+            for late in joined.gathers[4:]:
+                late.drain()
+        gradients(0, og_ref, act_ref, 0)
+
+    def second():
+        gradients(1, nf_ref, dgu_ref, 0)
+
+    def third():
+        gradients(2, nf_ref, dgu_ref, ff)
+        scatters[0].send()
 
     if joined is not None:
-        joined.activations_ready = activations_ready
+        joined.beside_feed_forward = (first, second, third)
         yield
     else:
-        activations_ready()
+        first()
         load.wait()
     dlow[...] = dot_nn(
         gb_ref[...].reshape(tokens, width), w_ref[:, pl.ds(*layout["out"])]
@@ -1555,8 +1436,10 @@
     if joined is None:
         for copy in early:
             copy.wait()
-    weights(1, nf_ref, dgu_ref, 0)
-    weights(2, nf_ref, dgu_ref, ff)
+        second()
+        third()
+    weights(3, gb_ref, low_ref, 0)
+    scatters[1].send()
     inner_rows = total.finish()
     for s in range(seqs):
         gate = z_ref[s].astype(F32)
@@ -1590,9 +1473,7 @@
         pass_refs[4:], True,
     )
     passing.start()
-    scatters[1].start()
-    weights(3, gb_ref, low_ref, 0)
-    steps(0)
+    scatters[3].start()
     @pl.loop(0, seqs)
     def _(s):
         x, state_in, state_out, step, _, running = parts(s)
@@ -1626,11 +1507,11 @@
         dbc[s, :, :size] = dot_tn(d_joined, state_out)
         dbc[s, :, size:] = dot_nn(d_joined, state_in) + dot_nt(low, entering[s])
 
+    scatters[2].send()
     passing.run()
-    scatters[2].start()
-    scatters[3].start()
     lane = iota((span, LANES), 1)
     upper = lane >= at_dim
+    even = lax.rem(at.t, 2) == 0
     if joined is None:
         rope_copy.wait()
     cosine, sine = rope_ref[:, :LANES], rope_ref[:, LANES:]
@@ -1661,28 +1542,41 @@
             query = q2_ref[s, pl.ds(h * span, span), :]
             d_keys = d_keys + dot_tn(d_score, query) + dot_tn(weight, moved)
             d_query.append(dot_nn(d_score, keys))
-        dkv[:, s] = d_keys.astype(BF16).reshape(devices, span, qw)
-        if joined is None and slots == 1 and s + 1 < seqs:
-            for copy in loads(s + 1):
-                copy.start()
+        d_keys = jnp.where(even, d_keys, pltpu.roll(d_keys, at_dim, 1))
+        turned = pltpu.roll(d_keys, at_dim, 1).reshape(devices, span, qw)
+        d_keys = d_keys.reshape(devices, span, qw)
+        if s < half:
+            dkv[:, s] = d_keys.astype(BF16)
+            dkv_other[:, s] = turned.astype(BF16)
+        else:
+            wide = iota((devices, span, qw), 2) < at_dim
+            kept_half = dkv[:, s - half].astype(F32)
+            dkv[:, s - half] = jnp.where(wide, kept_half, turned).astype(BF16)
+            kept_half = dkv_other[:, s - half].astype(F32)
+            dkv_other[:, s - half] = jnp.where(wide, kept_half, d_keys).astype(BF16)
         d_query = jnp.where(upper, pltpu.roll(d_query[1], at_dim, 1), d_query[0]) * scale
         d_in[pl.ds(s * span, span), pl.ds(*layout["q"])] = turn(
             d_query, cosine, -sine, at_dim // 2
         ).astype(BF16)
-    kv_scatter = LineScatter(
+    kv_scatter = DirectScatter(
         at,
         lambda k: dkv.at[k],
         lambda zz: dkv_got.at[zz],
-        None,
         lambda zz: dkv_line.at[zz],
         kv_sems,
         causal=True,
     )
+    kv_swap = remote(
+        dkv_other, dkv_swap, swap_sems.at[0], swap_sems.at[1], {"tensor": at.t_near}
+    )
+    kv_swap.start()
+    gradients(4, nx_ref, d_in, pieces[4][0])
+    kv_swap.wait()
+    dkv[...] = (dkv[...].astype(F32) + dkv_swap[...].astype(F32)).astype(BF16)
     kv_scatter.start()
-    steps(1)
+    scatters[3].send()
     finish(0)
-    weights(4, nx_ref, d_in, pieces[4][0])
-    scatters[4].start()
+    kv_scatter.send()
     passing.finish()
     tap_grads = [jnp.zeros((1, mixed), F32) for _ in range(4)]
     bias_grad = jnp.zeros((1, mixed), F32)
@@ -1711,7 +1605,7 @@
         d_decay = running_sum(d_running, backward=True)
         d_step = head_sums(d_xs * x, heads, head_dim) + d_decay * rate
         d_step = d_step * jax.nn.sigmoid(step_ref[s] + step_bias)
-        d_in[pl.ds(s * span, span), pl.ds(*layout["step"])] = d_step.astype(BF16)
+        d_in[pl.ds(s * span, span), pl.ds(*layout["ks"])] = pltpu.roll(d_step, at_dim, 1).astype(BF16)
         step_grad = step_grad + jnp.sum(d_step, 0, keepdims=True)
         decay_grad = decay_grad + jnp.sum(d_decay * step, 0, keepdims=True) * rate
         skip_grad = skip_grad + jnp.sum(dy[s] * x, 0, keepdims=True)
@@ -1756,33 +1650,40 @@
     sums[14:15, pl.ds(2 * LANES, LANES)] = head_sums(
         jnp.broadcast_to(skip_grad, (8, xw)), heads, head_dim
     )[:1]
-    steps(2)
-    kv_scatter.run_causal(dkv_own)
+    finish(1)
+    kv_scatter.finish(dkv_own)
     for s in range(seqs):
-        key_cosine = jnp.where(upper, 1.0, cosine)
-        key_sine = jnp.where(upper, 0.0, -sine)
-        d_in[pl.ds(s * span, span), pl.ds(*layout["kv"])] = turn(
-            dkv_own[s], key_cosine, key_sine, at_dim // 2
-        ).astype(BF16)
+        value = dkv_own[s % half]
+        value = value if s < half else pltpu.roll(value, at_dim, 1)
+        value = jnp.where(even, turn(value, cosine, -sine, at_dim // 2), value)
+        where = (pl.ds(s * span, span), pl.ds(*layout["ks"]))
+        d_in[where] = jnp.where(upper, d_in[where].astype(F32), value).astype(BF16)
+    value = ext_grad[:, pl.ds(8, span), :].reshape(tokens, mixed).astype(BF16)
+    d_in[:, pl.ds(*layout["x"])] = value[:, :xw]
+    d_in[:, pl.ds(*layout["state"])] = value[:, xw:]
+    halo_rows = jnp.concatenate([jnp.zeros((seqs, 8, mixed), F32), ext_grad[:, pl.ds(0, 8), :]], 1)
+    halo_rows = halo_rows.reshape(seqs * 16, mixed).astype(BF16)
+    rows_before = nxh_ref[...].reshape(seqs * 16, width)
+    halo_x, halo_state = halo_rows[:, :xw], halo_rows[:, xw:]
+    weights(5, nx_ref, d_in, pieces[5][0])
+    into = pl.ds(*layout["state"])
+    grads[:, into] = (grads[:, into].astype(F32) + dot_tn(rows_before, halo_state)).astype(BF16)
+    scatters[5].start()
+    weights(6, nx_ref, d_in, pieces[6][0])
+    into = pl.ds(*layout["x"])
+    grads[:, into] = (grads[:, into].astype(F32) + dot_tn(rows_before, halo_x)).astype(BF16)
+    scatters[6].start()
     pl.when(after)(lambda: halo().wait_recv())
-    ends = pl.ds(span, 8)
 
     @pl.when(after)
     def _():
-        ext_grad[:, ends, :] += halo_got[...]
-
-    value = ext_grad[:, pl.ds(8, span), :].reshape(tokens, mixed).astype(BF16)
-    d_in[:, pl.ds(layout["x"][0], mixed)] = value
-    back = RowScatter(
-        at,
-        rows_of(part),
-        lambda which, chunk: near.at[which, pl.ds(chunk * half, half)],
-        lambda chunk: far.at[pl.ds(chunk * half, half)],
-        send,
-        recv,
-    )
-    weights(5, nx_ref, d_in, pieces[5][0])
-    scatters[5].start()
+        ext_grad[:, pl.ds(span, 8), :] += halo_got[...]
+
+    for s in range(seqs):
+        value = ext_grad[s, pl.ds(span - 8, 16), :].astype(BF16)
+        ends = pl.ds(s * span + span - 16, 16)
+        d_in[ends, pl.ds(*layout["x"])] = value[:, :xw]
+        d_in[ends, pl.ds(*layout["state"])] = value[:, xw:]
     back = RowScatter(
         at,
         rows_of(part),
@@ -1795,13 +1696,9 @@
         value = dot_nt(d_in[pl.ds(c * rows, rows), :], w_ref[:, pl.ds(0, in_w)])
         part[pl.ds(c * half, half)] = value.astype(BF16).reshape(half, span, width)
         back.start(c)
-    weights(6, nx_ref, d_in, pieces[6][0])
-    scatters[6].start()
-    steps(3)
-    finish(1)
     for c in range(2):
         back.middle(c)
-    steps(4)
+    scatters[4].send()
     finish(2)
     total = jnp.zeros((1, width), F32)
     gain = gain_ref[...].reshape(1, width)
@@ -1831,57 +1728,50 @@
     finish(3)
     end(0)
     begin(1)
-    steps(5)
+    scatters[5].send()
     end(1)
     begin(2)
-    finish(4)
+    scatters[6].send()
     end(2)
     begin(3)
-    steps(6)
+    finish(4)
     end(3)
     finish(5)
-    kvw = layout["kv"][1]
-    kv_near[0, :, pl.ds(0, kvw)] = dw_ref[:, pl.ds(*layout["kv"])]
-    kv_near[0, :, pl.ds(kvw, sw)] = dw_ref[:, pl.ds(*layout["state"])]
+    kvw = layout["ks"][1]
+    kv_near[0, :, pl.ds(0, kvw)] = dw_ref[:, pl.ds(*layout["ks"])].astype(BF16)
+    kv_near[0, :, pl.ds(kvw, sw)] = dw_ref[:, pl.ds(*layout["state"])].astype(BF16)
     copy = remote(kv_near.at[0], kv_near.at[1], kv_send.at[0], kv_recv.at[0], {"tensor": at.t_near})
     copy.start()
     begin(4)
-    finish(6)
     copy.wait()
-    kv_far[0] = kv_near[0] + kv_near[1]
+    here, there = kv_near[0].astype(F32), kv_near[1].astype(F32)
+    keys = jnp.where(even, here[:, :kvw], there[:, :kvw])
+    values = jnp.where(even, there[:, :kvw], here[:, :kvw])
+    low_lanes = iota(keys.shape, 1) < at_dim
+    keys = jnp.where(low_lanes, keys, pltpu.roll(values, at_dim, 1))
+    kv_far[0, :, :kvw] = keys.astype(BF16)
+    kv_far[0, :, kvw:] = (here[:, kvw:] + there[:, kvw:]).astype(BF16)
     copy = remote(kv_far.at[0], kv_far.at[1], kv_send.at[1], kv_recv.at[1], {"tensor": at.t_far})
     copy.start()
     end(4)
     for i in range(5, len(exchanges)):
         begin(i)
         end(i)
+    finish(6)
     copy.wait()
-    kvs[:, pl.ds(0, kvw)] = kv_far[0, :, pl.ds(0, kvw)]
-    kvs[:, pl.ds(kvw, kvw)] = kv_far[1, :, pl.ds(0, kvw)]
-
-    @pl.when(at.t >= 2)
-    def _():
-        kvs[:, pl.ds(0, kvw)] = kv_far[1, :, pl.ds(0, kvw)]
-        kvs[:, pl.ds(kvw, kvw)] = kv_far[0, :, pl.ds(0, kvw)]
-
-    kvs[:, pl.ds(2 * kvw, sw)] = kv_far[0, :, pl.ds(kvw, sw)] + kv_far[1, :, pl.ds(kvw, sw)]
+    own_first = at.t < 2
+    for k in range(2):
+        mine_first = own_first if k == 0 else jnp.logical_not(own_first)
+        kvs[:, pl.ds(k * kvw, kvw)] = jnp.where(
+            mine_first, kv_far[0, :, :kvw], kv_far[1, :, :kvw]
+        ).astype(F32)
+    kvs[:, pl.ds(2 * kvw, sw)] = kv_far[0, :, kvw:].astype(F32) + kv_far[1, :, kvw:].astype(F32)
     for scatter in [*scatters, kv_scatter]:
         scatter.drain()
     for c in range(2):
         back.drain(c)
     pl.when(before)(lambda: halo().wait_send())
     yield
-
-
-def scatter_sems(devices, pieces):
-    dma = pltpu.SemaphoreType.DMA
-    out = []
-    for _, _, cross in pieces:
-        if cross:
-            out += [dma((2,))] + [dma((devices,)) for _ in range(4)]
-        else:
-            out += line_scatter_sems(devices)
-    return out
 
 
 def back_specs(cfg, joined=False):
@@ -1893,13 +1783,12 @@
     depth = width // devices
     lines = devices // 2
     columns = layout["down"][0] + layout["down"][1]
-    xw, sw, qw, kvw = (layout[k][1] for k in ("x", "state", "q", "kv"))
+    xw, sw, qw, kvw = (layout[k][1] for k in ("x", "state", "q", "ks"))
     size = sw // 2
     mixed = xw + sw
     in_w = layout["in"][1]
     own = (seqs, sub, width)
     rounds = devices.bit_length() - 1
-    crossed = max(LANES, sum(piece[1] for piece in pieces if piece[2]))
     slots = 2 if devices * span <= 2048 else 1
     dma = pltpu.SemaphoreType.DMA
     outs = (
@@ -1921,24 +1810,26 @@
         "after_state": pltpu.VMEM((seqs, size, xw), BF16),
         "keys_buf": pltpu.VMEM((slots, devices, span, qw), BF16),
         "prob_buf": pltpu.VMEM((slots, 2 * span, devices * span), BF16),
-        "dkv": pltpu.VMEM((devices, seqs, span, qw), BF16),
-        "dkv_got": pltpu.VMEM((lines, seqs, span, qw), BF16),
-        "dkv_line": pltpu.VMEM((lines, seqs, span, qw), BF16),
-        "dkv_own": pltpu.VMEM((seqs, span, qw), F32),
+        "dkv": pltpu.VMEM((devices, half, span, qw), BF16),
+        "dkv_other": pltpu.VMEM((devices, half, span, qw), BF16),
+        "dkv_swap": pltpu.VMEM((devices, half, span, qw), BF16),
+        "dkv_got": pltpu.VMEM((lines, half, span, qw), BF16),
+        "dkv_line": pltpu.VMEM((lines, half, span, qw), BF16),
+        "dkv_own": pltpu.VMEM((half, span, qw), F32),
         "part": pltpu.VMEM((seqs, span, width), BF16),
         "near": pltpu.VMEM((2,) + own, BF16),
         "far": pltpu.VMEM(own, BF16),
         "grads": pltpu.VMEM((width, layout["gu"][0] if joined else columns), BF16),
         "got": pltpu.VMEM((lines * depth, columns), BF16),
-        "line": pltpu.VMEM(((lines + 1) * depth, columns), BF16),
-        "line2": pltpu.VMEM(((lines + 1) * 2 * depth, crossed), BF16),
+        "line": pltpu.VMEM((lines * depth, columns), BF16),
         "small_near": pltpu.VMEM((8, width), F32),
         "small_far": pltpu.VMEM((8, width), F32),
         "small_dp": pltpu.VMEM((rounds, 16, width), F32),
-        "kv_near": pltpu.VMEM((2, depth, kvw + sw), F32),
-        "kv_far": pltpu.VMEM((2, depth, kvw + sw), F32),
+        "kv_near": pltpu.VMEM((2, depth, kvw + sw), BF16),
+        "kv_far": pltpu.VMEM((2, depth, kvw + sw), BF16),
         "sq_own": pltpu.VMEM((8, span), F32),
         "sq_got": pltpu.VMEM((3, 8, span), F32),
+        "swap_sems": dma((2,)),
         "rope": pltpu.VMEM((span, 2 * LANES), F32),
         "w_sem": dma,
         "early_sems": dma((2,)),
@@ -1958,8 +1849,7 @@
     }
     rest = (
         state_pass_scratch(half, size, xw)
-        + line_scatter_sems(devices)
-        + scatter_sems(devices, pieces)
+        + scatter_sems(devices) * (1 + len(pieces))
     )
     return outs, scratch, rest
 
@@ -1978,7 +1868,7 @@
     outs, scratch, rest = back_specs(cfg)
     vmem = pl.BlockSpec(memory_space=pltpu.VMEM)
     in_specs = [vmem] * (1 + len(args))
-    for i in (3, 8, 9, 11, 13, 25):
+    for i in (3, 8, 9, 11, 13, 27):
         in_specs[i] = pl.BlockSpec(memory_space=pl.ANY)
     return pl.pallas_call(
         partial(run_back, cfg),
@@ -2001,11 +1891,12 @@
 
 def joined_kernel(cfg, *refs):
     devices, layout = cfg["devices"], cfg["layout"]
-    inputs, refs = refs[:21], refs[21:]
-    dn_in, fgain_ref = inputs[19:]
+    inputs, refs = refs[:23], refs[23:]
+    dn_in, fgain_ref = inputs[21:]
     x_ref, og_in, gain_ref = inputs[:3]
-    rope_any, xt_ref, _, stt_ref, _, head_ref, mgain_ref = inputs[12:19]
-    inputs = inputs[:19]
+    rope_any, xt_ref, _, stt_ref = inputs[12:16]
+    mgain_ref = inputs[20]
+    inputs = inputs[:21]
     block_out, rg, dw, sums, kvs = refs[:5]
     refs = refs[5:]
 
@@ -2024,18 +1915,18 @@
     names = [name for name in scratch if name not in APART]
     mine = dict(zip(names, take(len(names))))
     mine["part"] = fed_scratch[0]
-    mine["rope"] = mixed_scratch[3]
+    mine["rope"] = mixed_scratch[5]
     back_scratch = [mine.get(name) for name in scratch] + list(take(len(rest)))
     (
         w_all, nx, og, low, kv, q2, probs, att, ext, pre, step_buf, entering, carry, y_buf, z_buf,
-        squares, aux_ref, seg_rows,
+        squares, aux_ref, seg_rows, head_ref, nxh,
     ) = mixed
     _, gh, gb, nf, act, dgu, gain_part = fed
     joined = Joined(dn_in)
     later = back_kernel(
         cfg, x_ref, gh, gain_ref, w_all, nx, og, gb, low, nf, dgu, act, kv, q2, probs, att, ext, pre,
-        step_buf, entering, carry, y_buf, z_buf, squares, aux_ref, seg_rows, rope_any, xt_ref, stt_ref,
-        head_ref, mgain_ref, gain_part, rg, dw, sums, kvs, *back_scratch, joined=joined,
+        step_buf, entering, carry, y_buf, z_buf, squares, aux_ref, seg_rows, head_ref, nxh, rope_any, xt_ref,
+        stt_ref, mgain_ref, gain_part, rg, dw, sums, kvs, *back_scratch, joined=joined,
     )
     mixer_kernel(cfg, *inputs, *mixed, *mixed_scratch, joined=joined)
     next(later)
@@ -2087,7 +1978,7 @@
     xw, sw = layout["x"][1], layout["state"][1]
     qw = layout["q"][1]
     ff = layout["down"][1]
-    kvw = layout["kv"][1]
+    kvw = layout["ks"][1]
 
     def part(name):
         return dw[:, pl.ds(*layout[name])]
@@ -2104,7 +1995,7 @@
     wmi[:, 0, :] = part("z")
     wmi[:, 1, :] = part("x")
     wst[...] = kvs[:, 2 * kvw :]
-    wsp[...] = part("step")[:, :local]
+    wsp[...] = part("ks").T[kvw // 2 : kvw // 2 + local, :]
     gate_up = part("gu")
     wgu[:, 0, :] = gate_up[:, :ff]
     wgu[:, 1, :] = gate_up[:, ff:]
@@ -2121,7 +2012,7 @@
 def unpack(layout, local, dw, kvs, sums, rg, block):
     depth = dw.shape[0]
     width = sums.shape[1]
-    xw, sw, qw, ff, kvw = (layout[k][1] for k in ("x", "state", "q", "down", "kv"))
+    xw, sw, qw, ff, kvw = (layout[k][1] for k in ("x", "state", "q", "down", "ks"))
 
     def shape(*dims):
         return jax.ShapeDtypeStruct(dims, F32)
@@ -2136,7 +2027,7 @@
         shape(qw, depth),
         shape(depth, 2, xw),
         shape(depth, sw),
-        shape(depth, local),
+        shape(local, depth),
         shape(4, xw),
         shape(xw),
         shape(4, sw),
@@ -2203,10 +2094,9 @@
     layout = {}
     columns = 0
     for name, size in (
+        ("state", state_width),
+        ("ks", 2 * head_dim),
         ("x", mixer_width),
-        ("state", state_width),
-        ("step", LANES),
-        ("kv", 2 * head_dim),
         ("q", query_width),
         ("z", mixer_width),
         ("out", query_width + mixer_width),
@@ -2216,34 +2106,35 @@
         layout[name] = (columns, size)
         columns += size
     layout["in"] = (0, layout["out"][0])
-    kv_at, q_at, gu_at = (layout[k][0] for k in ("kv", "q", "gu"))
+    q_at, gu_at = (layout[k][0] for k in ("q", "gu"))
     config = {
         "devices": shard_count,
         "layout": layout,
         "heads": mixer_local,
         "rows": resid_in.shape,
         "pieces": (
-            (0, kv_at, False),
-            (kv_at, layout["out"][0] - kv_at, False),
-            (*layout["out"], True),
-            (*layout["gu"], False),
+            (0, layout["x"][0], False),
+            (*layout["x"], False),
+            (q_at, layout["out"][0] - q_at, False),
+            (*layout["out"], False),
+            (gu_at, ff, False),
+            (gu_at + ff, ff, False),
         ),
         "scatters": (
-            (*layout["down"], False),
-            (gu_at, ff, False),
-            (gu_at + ff, ff, False),
-            (*layout["out"], True),
-            (q_at, layout["out"][0] - q_at, False),
-            (layout["state"][0], q_at - layout["state"][0], False),
-            (*layout["x"], False),
+            layout["down"],
+            (gu_at, ff),
+            (gu_at + ff, ff),
+            layout["out"],
+            (q_at, layout["out"][0] - q_at),
+            (0, layout["x"][0]),
+            layout["x"],
         ),
     }
 
-    def lanes(array):
-        return jnp.pad(array, (0, LANES - array.shape[0]))
-
-    head_rows = jnp.stack([lanes(step_bias), lanes(decay_log), lanes(skip_gain)])
     rope = jnp.asarray(rope_table(segment_ids.shape[1], head_dim))
+    def results(outs):
+        return (*outs[:9], outs[9].T, *outs[10:])
+
     raw = (
         resid_in,
         out_grad,
@@ -2252,7 +2143,7 @@
         keyvalue_weight,
         mixer_input_weight,
         state_input_weight,
-        step_weight,
+        step_weight.T,
         gate_up_weight,
         attention_output_weight,
         mixer_output_weight,
@@ -2262,7 +2153,9 @@
         conv_mixer_bias,
         conv_state,
         conv_state_bias,
-        head_rows,
+        step_bias,
+        decay_log,
+        skip_gain,
         mixer_gain,
     )
     if segment_ids.size <= JOINED_TOKENS:
@@ -2270,12 +2163,13 @@
         block_out, resid_grad, weight_grads, sums, replicated = joined_layer(
             config, *raw, down_weight, ffn_gain
         )
-        return unpack(
-            layout, mixer_local, weight_grads, replicated, sums, resid_grad, block_out
+        return results(
+            unpack(layout, mixer_local, weight_grads, replicated, sums, resid_grad, block_out)
         )
     (
         w_all, span_normed_input, span_gradient, branch_low, keys, queries, probs, attention, ext,
-        pre, step_pre, entering, state_decay, mixer_y, gate_z, squares, aux, seg_rows,
+        pre, step_pre, entering, state_decay, mixer_y, gate_z, squares, aux, seg_rows, head_rows,
+        rows_before,
     ) = mixer(config, *raw)
     block_out, grad_hidden, grad_branch, span_feedforward, activated, grad_gate_up, ffn_gain_part = (
         feed_forward(
@@ -2316,14 +2210,17 @@
         squares,
         aux,
         seg_rows,
+        head_rows,
+        rows_before,
         rope,
         conv_mixer,
         conv_state,
-        head_rows,
         mixer_gain,
         ffn_gain_part,
     )
-    return unpack(layout, mixer_local, weight_grads, replicated, sums, resid_grad, block_out)
+    return results(
+        unpack(layout, mixer_local, weight_grads, replicated, sums, resid_grad, block_out)
+    )
 
 
 def solution(mesh):

time: 283 us -> 239 us (0.84)
  Pallas kernels: 277 us -> 237 us
  local copies, waits for them, and re-layouts: 4.25 us -> 0 us
    pallas_call x1, Pallas kernels: 273 us -> 233 us  [joined_layer(): pl.pallas_call(partial(joined_kernel, cfg), out_shape=tuple((jax.ShapeDty...]
where the time goes in v1:
time: 239 us; the launch traced here: 238 us
  Pallas kernels  237 us (99%)
    pallas_call x1, Pallas kernels, joined_layer(): pl.pallas_call(partial(joined_kernel, cfg), out_shape=tuple((jax.ShapeDty...  233 us

profile of v1, /device:TPU:0, one launch (start us, length us, event | category | flops | bytes accessed | tf_op | source)
XLA Modules:
  0.0 237.7 jit_solution(3053963957611714593)
XLA Ops:
  0.7 233.4 %layer.1 = (bf16[4,32,1024]{2,1,0:T(8,128)(2,1)}, f32[4,32,1024]{2,1,0:T(8,128)}, f32[128,3328]{1,0:T(8,128)}, f32[16,1024]{1,0:T(8,128)}, f32[128,512]{1,0:T(8,128)}) custom-call(bf16[4,32,1024]{2,1,0:T(8,128)(2,1)} %refs_0_.1, bf16[4,32,1024]{2,1,0:T(8,128)(2,1)} %refs_1_.1, f32[1024]{0:T(1024)} %refs_2_.1, bf16[128,128]{1,0:T(8,128)(2,1)} %refs_3_.1, ...), custom_call_target="tpu_custom_call" | custom-call | tf_op jit(solution)/shard_map/layer/pallas_call | solution.py:1950
  234.1 3.4 %unpack.1 = (bf16[4,32,1024]{2,1,0:T(8,128)(2,1)}, f32[4,32,1024]{2,1,0:T(8,128)}, f32[1024]{0:T(1024)}, f32[1024]{0:T(1024)}, f32[128,128]{1,0:T(8,128)}, /*ind...) custom-call(f32[128,3328]{1,0:T(8,128)} %get-tuple-element.47.refs_0, ...), custom_call_target="tpu_custom_call" | custom-call | tf_op jit(solution)/shard_map/unpack/pallas_call | solution.py:2044
